TPU v7x, 32 devices: a whole 2x2x4 slice. The times are simulated.
32 devices in a mesh: clip: 4 (over z), frame: 4 (over y, x), seg: 2 (over core).
Axes of the slice: x: 2, y: 2, z: 4, core: 2. Of those that a mesh axis runs over, the one named last changes fastest.
Arguments:
- video: bfloat16 [2, 40, 4, 197, 384], P(None, ('clip', 'seg'), 'frame'), may hold values from -6 to 6
- captions: bfloat16 [2, 8, 128, 384], P(None, ('clip', 'seg'), 'frame'), may hold values from -6 to 6
- caption_lengths: int32 [2, 8, 9], P(None, ('clip', 'seg')), may hold values from 1 to 64, 128 in all within a row
- message_weight: bfloat16 [384, 384], replicated, may hold values from -0.3125 to 0.3125
- message_gain: float32 [384], replicated, may hold values from 0.25 to 1.75
- qkv_weights: bfloat16 [3, 3, 384, 384], replicated, may hold values from -0.3125 to 0.3125
- out_weights: bfloat16 [3, 384, 384], replicated, may hold values from -0.875 to 0.875
- mlp_up: bfloat16 [384, 1536], replicated, may hold values from -0.3125 to 0.3125
- mlp_down: bfloat16 [1536, 384], replicated, may hold values from -0.15625 to 0.15625
- gains: float32 [4, 384], replicated, may hold values from 0.5 to 1.5
- video_cot: bfloat16 [2, 40, 4, 197, 384], P(None, ('clip', 'seg'), 'frame'), may hold values from -6 to 6
- caption_cot: bfloat16 [2, 8, 128, 384], P(None, ('clip', 'seg'), 'frame'), may hold values from -6 to 6
Outputs:
- video_out: bfloat16 [2, 40, 4, 197, 384], P(None, ('clip', 'seg'), 'frame')
- caption_out: bfloat16 [2, 8, 128, 384], P(None, ('clip', 'seg'), 'frame')
- video_grad: bfloat16 [2, 40, 4, 197, 384], P(None, ('clip', 'seg'), 'frame')
- caption_grad: bfloat16 [2, 8, 128, 384], P(None, ('clip', 'seg'), 'frame')
- message_weight_grad: float32 [384, 384], replicated
- message_gain_grad: float32 [384], replicated
- qkv_weights_grad: float32 [3, 3, 384, 384], replicated
- out_weights_grad: float32 [3, 384, 384], replicated
- mlp_up_grad: float32 [384, 1536], replicated
- mlp_down_grad: float32 [1536, 384], replicated
- gains_grad: float32 [4, 384], replicated
Inputs may be any that keep to these rules, and one draw needn't show every extreme that they name: `caption_lengths`: the entries of each row sum to 128; the last entry is the padding at the end of the pack, the others are the lengths of its captions; caption j of a pack describes clip j mod 5 of its group.
All inputs are finite; a program needn't handle non-finite values.
Results may differ from a plain program's by a relative error of at most 0.019.
Values may be sent and summed in bfloat16 or wider, within the bound.
No kernel may reach another device: no remote copies, remote signals or barrier semaphores. Data moves between devices by JAX's collectives and lax.ppermute only.
A program may use at most 192 MiB of HBM per device.

v0:
```python
import functools

import jax
import jax.numpy as jnp
from jax import lax
from jax.experimental import pallas as pl
from jax.experimental.pallas import tpu as pltpu
from jax.sharding import PartitionSpec as P

HEADS = 6
HEAD_DIM = 64
EPS = 1e-05
SCALE = 0.125
MASKED = -1e30

f32 = jnp.float32
bf16 = jnp.bfloat16


def nn(a, b):
    return lax.dot_general(a, b, (((1,), (0,)), ((), ())), preferred_element_type=f32)


def nt(a, b):
    return lax.dot_general(a, b, (((1,), (1,)), ((), ())), preferred_element_type=f32)


def tn(a, b):
    return lax.dot_general(a, b, (((0,), (0,)), ((), ())), preferred_element_type=f32)


def exact(a, b):
    return lax.dot_general(
        a, b, (((1,), (0,)), ((), ())), precision=lax.Precision.HIGHEST, preferred_element_type=f32
    )


def unit_norm(x):
    center = x - jnp.mean(x, axis=-1, keepdims=True)
    inv = lax.rsqrt(jnp.mean(center * center, axis=-1, keepdims=True) + EPS)
    return center * inv, inv


def norm_back(unit, inv, gain, dy):
    du = dy * gain
    mean_du = jnp.mean(du, axis=-1, keepdims=True)
    mean_dot = jnp.mean(du * unit, axis=-1, keepdims=True)
    return inv * (du - mean_du - unit * mean_dot)


def row_sum(x):
    return jnp.sum(x, axis=0, keepdims=True)


def sigmoid(x):
    return 0.5 + 0.5 * jnp.tanh(0.5 * x)


def head_mask(shape, lane_dim, head):
    lane = lax.broadcasted_iota(jnp.int32, shape, lane_dim)
    return (lane >= head * HEAD_DIM) & (lane < (head + 1) * HEAD_DIM)


def head_columns(width):
    lane = lax.broadcasted_iota(jnp.int32, (width, 128), 0)
    col = lax.broadcasted_iota(jnp.int32, (width, 128), 1)
    return ((lane >= col * HEAD_DIM) & (lane < (col + 1) * HEAD_DIM)).astype(f32)


def head_rows(width):
    col = lax.broadcasted_iota(jnp.int32, (128, width), 0)
    lane = lax.broadcasted_iota(jnp.int32, (128, width), 1)
    return ((lane >= col * HEAD_DIM) & (lane < (col + 1) * HEAD_DIM)).astype(f32)


def pad_rows(x, rows):
    if x.shape[0] == rows:
        return x
    return jnp.concatenate([x, jnp.zeros((rows - x.shape[0], x.shape[1]), x.dtype)], axis=0)


def put_row(block, at, row):
    top = at // 16 * 16
    tail = block[top : top + 16]
    index = lax.broadcasted_iota(jnp.int32, tail.shape, 0)
    tail = jnp.where(index == at - top, row, tail)
    pieces = [tail]
    if top:
        pieces.insert(0, block[:top])
    if top + 16 < block.shape[0]:
        pieces.append(block[top + 16 :])
    return jnp.concatenate(pieces, axis=0) if len(pieces) > 1 else tail


def full(shape):
    return pl.BlockSpec(shape, lambda *_: (0,) * len(shape))


def frame_block(shape):
    return pl.BlockSpec((1,) + shape, lambda i, *_: (i, 0, 0))


def frames_block(batch, shape):
    return pl.BlockSpec((batch,) + shape, lambda i, *_: (i, 0, 0))


def stagger(jobs, stages, gap):
    for at in range(len(jobs) + (len(stages) - 1) * gap):
        for k, stage in enumerate(stages):
            j = at - k * gap
            if 0 <= j < len(jobs):
                stage(jobs[j])


def share_of(count, most):
    return max(b for b in range(1, most + 1) if count % b == 0)


def square(width, *at):
    return pl.BlockSpec((None,) * len(at) + (width, width), lambda *_: at + (0, 0))


def scalars():
    return pl.BlockSpec(memory_space=pltpu.SMEM)


def shape_of(shape, dtype):
    return jax.ShapeDtypeStruct(shape, dtype)


def params(mib):
    return pltpu.CompilerParams(vmem_limit_bytes=mib * 1024 * 1024)


def cost(flops, nbytes):
    return pl.CostEstimate(flops=int(flops), bytes_accessed=int(nbytes), transcendentals=0)


def class_kernel(video_ref, out_ref):
    clips, _, micro, width = video_ref.shape
    rows = [video_ref[c, 0, m : m + 1, :].astype(f32) for m in range(micro) for c in range(clips)]
    out_ref[...] = pad_rows(jnp.concatenate(rows, axis=0), out_ref.shape[0]).astype(bf16)


def class_rows(video, slots):
    micro, clips, per_frame, patch, width = video.shape
    turned = video.transpose(1, 2, 3, 0, 4).reshape(clips * per_frame, patch, micro, width)
    return pl.pallas_call(
        class_kernel,
        grid=(1,),
        in_specs=[pl.BlockSpec((clips * per_frame, 1, micro, width), lambda i: (0, 0, 0, 0))],
        out_specs=full((slots, width)),
        out_shape=shape_of((slots, width), bf16),
        name="class_rows",
    )(turned)


def norm_kernel(video_ref, gains_ref, wk_ref, wv_ref, normed_ref, kv_ref, wkv):
    batch, rows, width = normed_ref.shape

    @pl.when(pl.program_id(0) == 0)
    def _():
        wkv[:, :width] = wk_ref[...]
        wkv[:, width:] = wv_ref[...]

    parts = []
    for i in range(batch):
        unit, _ = unit_norm(video_ref[i].astype(f32))
        parts.append(pad_rows(unit * gains_ref[0:1, :], rows).astype(bf16))
        normed_ref[i] = parts[i]
    normed = jnp.concatenate(parts, axis=0)
    kv_ref[...] = nn(normed, wkv[...]).astype(bf16).reshape(batch, rows, 2 * width)


def norm_tokens(video, gains, qkv, rows):
    count, patch, width = video.shape
    batch = share_of(count, 5)
    return pl.pallas_call(
        norm_kernel,
        grid=(count // batch,),
        in_specs=[
            frames_block(batch, (patch, width)),
            full(gains.shape),
            square(width, 1, 1),
            square(width, 1, 2),
        ],
        out_specs=[
            frames_block(batch, (rows, width)),
            frames_block(batch, (rows, 2 * width)),
        ],
        out_shape=[
            shape_of((count, rows, width), bf16),
            shape_of((count, rows, 2 * width), bf16),
        ],
        scratch_shapes=[pltpu.VMEM((width, 2 * width), bf16)],
        compiler_params=params(20),
        cost_estimate=cost(4 * count * rows * width * width, 8 * count * rows * width),
        name="norm_tokens",
    )(video, gains, qkv, qkv)


def message_scores(query, keys, columns):
    return [exact(query.astype(f32) * key.astype(f32), columns) * SCALE for key in keys]


def message_probs(scores):
    top = functools.reduce(jnp.maximum, scores)
    expo = [jnp.exp(score - top) for score in scores]
    total = functools.reduce(jnp.add, expo)
    return [e / total for e in expo]


def first_kernel(
    pieces, count, tokens, *refs
):
    gathered = refs[:pieces]
    (
        mw_ref, mg_ref, qkv_ref, outw_ref, up_ref, down_ref, gains_ref, kv_ref,
        message_ref, nmsg_ref, kvmsg_ref, visual_ref, final_ref, ctx,
    ) = refs[pieces:]
    width = mw_ref.shape[0]
    slots = gathered[0].shape[0]
    rows = kv_ref.shape[1]
    classes = jnp.concatenate([g[...] for g in gathered], axis=0)
    start = nn(classes, mw_ref[...]).astype(bf16)
    unit, _ = unit_norm(start.astype(f32))
    normed = (unit * mg_ref[...]).astype(bf16)
    keys = nn(normed, qkv_ref[0, 1]).astype(bf16)
    values = nn(normed, qkv_ref[0, 2]).astype(bf16)
    query = nn(normed[:slots], qkv_ref[0, 0]).astype(bf16)
    columns, spread = head_columns(width), head_rows(width).astype(bf16)
    cut = [slice(g * slots, (g + 1) * slots) for g in range(pieces)]
    probs = message_probs(message_scores(query, [keys[c] for c in cut], columns))
    context = functools.reduce(
        jnp.add,
        [nn(p.astype(bf16), spread) * values[c].astype(f32) for p, c in zip(probs, cut)],
    ).astype(bf16)
    message = start[:slots].astype(f32) + nn(context, outw_ref[0])
    message_ref[...] = message
    unit, _ = unit_norm(message)
    nmsg = (unit * gains_ref[0:1, :]).astype(bf16)
    nmsg_ref[...] = nmsg.astype(f32)
    kmsg = nn(nmsg, qkv_ref[1, 1]).astype(bf16).astype(f32)
    vmsg = nn(nmsg, qkv_ref[1, 2]).astype(bf16).astype(f32)

    own = gathered[0][...].astype(f32)
    unit, _ = unit_norm(own)
    qcls = nn((unit * gains_ref[0:1, :]).astype(bf16), qkv_ref[1, 0]).astype(bf16).astype(f32) * SCALE
    head = lax.broadcasted_iota(jnp.int32, (16, width), 0)
    lane = lax.broadcasted_iota(jnp.int32, (16, width), 1)
    mine = (lane >= head * HEAD_DIM) & (lane < (head + 1) * HEAD_DIM)
    token = lax.broadcasted_iota(jnp.int32, (16, rows), 1)
    ctx[...] = jnp.zeros(ctx.shape, f32)
    kvmsg_ref[:, :width] = kmsg
    kvmsg_ref[:, width:] = vmsg
    queries = [jnp.where(mine, qcls[i : i + 1], 0.0) for i in range(count)]
    scores = [nt(queries[i].astype(bf16), kv_ref[i, :, :width]) for i in range(count)]
    probs = []
    for i in range(count):
        last = jnp.sum(queries[i] * kmsg[i : i + 1], axis=1, keepdims=True)
        score = jnp.where(token == tokens - 1, last, scores[i])
        score = jnp.where(token < tokens, score, MASKED)
        expo = jnp.exp(score - jnp.max(score, axis=1, keepdims=True))
        probs.append((expo / jnp.sum(expo, axis=1, keepdims=True)).astype(bf16))
    outs = [nn(probs[i], kv_ref[i, :, width:]) for i in range(count)]
    for i in range(count):
        extra = jnp.sum(
            jnp.where(token == tokens - 1, probs[i].astype(f32), 0.0), axis=1, keepdims=True
        )
        out = outs[i] + extra * vmsg[i : i + 1]
        ctx[i : i + 1, :] = row_sum(jnp.where(mine, out, 0.0))
    resid = own + nn(ctx[...].astype(bf16), outw_ref[1])
    unit, _ = unit_norm(resid)
    hidden = nn((unit * gains_ref[1:2, :]).astype(bf16), up_ref[...])
    active = (hidden * sigmoid(1.702 * hidden)).astype(bf16)
    final = resid + nn(active, down_ref[...])
    final_ref[...] = final
    unit, _ = unit_norm(final)
    visual_ref[...] = (unit * gains_ref[2:3, :]).astype(bf16)


def first_rows(gathered, mw, mg, qkv, outw, up, down, gains, kv, tokens):
    count, width = kv.shape[0], mw.shape[0]
    slots = gathered[0].shape[0]
    operands = list(gathered) + [mw, mg, qkv, outw, up, down, gains, kv]
    return pl.pallas_call(
        functools.partial(first_kernel, len(gathered), count, tokens),
        grid=(1,),
        in_specs=[full(x.shape) for x in gathered]
        + [
            full(mw.shape),
            full(mg.shape),
            pl.BlockSpec((2, 3, width, width), lambda i: (0, 0, 0, 0)),
            pl.BlockSpec((2, width, width), lambda i: (0, 0, 0)),
            full(up.shape),
            full(down.shape),
            full(gains.shape),
            full(kv.shape),
        ],
        out_specs=[full((slots, width))] * 2 + [full((slots, 2 * width))] + [full((slots, width))] * 2,
        out_shape=[
            shape_of((slots, width), f32),
            shape_of((slots, width), f32),
            shape_of((slots, 2 * width), f32),
            shape_of((slots, width), bf16),
            shape_of((slots, width), f32),
        ],
        scratch_shapes=[pltpu.VMEM((slots, width), f32)],
        compiler_params=params(16),
        cost_estimate=cost(4e9, 12e6),
        name="first_rows",
    )(*operands)


def with_message(block, rows_ref, tokens, frame):
    top = (tokens - 1) // 16 * 16
    tail = block[top : top + 16].astype(f32)
    index = lax.broadcasted_iota(jnp.int32, tail.shape, 0)
    tail = jnp.where(index == tokens - 1 - top, rows_ref[pl.ds(frame, 1), :], tail).astype(bf16)
    pieces = [block[:top], tail]
    if top + 16 < block.shape[0]:
        pieces.append(block[top + 16 :])
    return jnp.concatenate(pieces, axis=0)


def masked_tail(scores, tokens):
    top = tokens // 16 * 16
    if top >= scores.shape[0]:
        return scores
    tail = scores[top:]
    index = lax.broadcasted_iota(jnp.int32, tail.shape, 0)
    return jnp.concatenate([scores[:top], jnp.where(index < tokens - top, tail, MASKED)], axis=0)


def half_pair(block_t, head):
    own = block_t[head * HEAD_DIM : (head + 1) * HEAD_DIM]
    none = jnp.zeros(own.shape, own.dtype)
    return jnp.concatenate([own, none] if head % 2 == 0 else [none, own], axis=0)


def pair_lanes(block, head):
    at = head // 2 * 2 * HEAD_DIM
    return block[:, at : at + 2 * HEAD_DIM]


def attend_kernel(
    tokens, normed_ref, kv_ref, video_ref, message_ref, nmsg_ref, kvmsg_ref, wq_ref, wv_ref, wo_ref,
    *refs,
):
    resid_ref, ctx_ref, lse_ref, wqt, wvt = refs[-5:]
    step = pl.program_id(0)

    @pl.when(step == 0)
    def _():
        wqt[...] = wq_ref[...].T
        wvt[...] = wv_ref[...].T

    batch, rows, width = normed_ref.shape
    normed, keys = [], []
    for i in range(batch):
        frame = step * batch + i
        normed.append(with_message(normed_ref[i], nmsg_ref, tokens, frame))
        keys.append(with_message(kv_ref[i], kvmsg_ref, tokens, frame))
    queries_t = [nt(wqt[...], n).astype(bf16) * jnp.bfloat16(SCALE) for n in normed]
    values_t = [nt(wvt[...], n).astype(bf16) for n in normed]
    jobs = [(i, h) for i in range(batch) for h in range(HEADS)]
    contexts, stats, scores, expos, totals = {}, {}, {}, {}, {}

    def score(job):
        i, head = job
        scores[job] = nn(pair_lanes(keys[i], head), half_pair(queries_t[i], head))

    def soften(job):
        one = masked_tail(scores.pop(job), tokens)
        top = jnp.max(one, axis=0, keepdims=True)
        expo = jnp.exp(one - top)
        totals[job] = row_sum(expo)
        expos[job] = expo.astype(bf16)
        stats[job] = top + jnp.log(totals[job])

    def mix(job):
        i, head = job
        own = values_t[i][head * HEAD_DIM : (head + 1) * HEAD_DIM]
        contexts[job] = nn(own, expos.pop(job)) * (1.0 / totals[job])

    stagger(jobs, [score, soften, mix], 3)
    for i in range(batch):
        context_t = jnp.concatenate([contexts[i, h] for h in range(HEADS)], axis=0).astype(bf16)
        ctx_ref[i] = context_t
        pad = [jnp.zeros((8 - HEADS, rows), f32)]
        lse_ref[i] = jnp.concatenate([stats[i, h] for h in range(HEADS)] + pad, axis=0)
        row = message_ref[pl.ds(step * batch + i, 1), :]
        base = put_row(pad_rows(video_ref[i].astype(f32), rows), tokens - 1, row)
        resid_ref[i] = base + tn(context_t, wo_ref[...])


def attend(normed, kv, video, message, nmsg, kvmsg, qkv, outw, tokens, after=()):
    count, rows, width = normed.shape
    slots = message.shape[0]
    batch = share_of(count, 2)
    return pl.pallas_call(
        functools.partial(attend_kernel, tokens),
        grid=(count // batch,),
        in_specs=[
            frames_block(batch, (rows, width)),
            frames_block(batch, (rows, 2 * width)),
            frames_block(batch, video.shape[1:]),
            full((slots, width)),
            full((slots, width)),
            full((slots, 2 * width)),
            square(width, 1, 0),
            square(width, 1, 2),
            square(width, 1),
        ]
        + [pl.BlockSpec(memory_space=pl.ANY)] * len(after),
        out_specs=[
            frames_block(batch, (rows, width)),
            frames_block(batch, (width, rows)),
            frames_block(batch, (8, rows)),
        ],
        out_shape=[
            shape_of((count, rows, width), f32),
            shape_of((count, width, rows), bf16),
            shape_of((count, 8, rows), f32),
        ],
        scratch_shapes=[pltpu.VMEM((width, width), bf16)] * 2,
        compiler_params=params(20),
        cost_estimate=cost(14e9, 10e6),
        name="attend",
    )(normed, kv, video, message, nmsg, kvmsg, qkv, qkv, outw, *after)


def caption_kernel(
    pieces, groups, clips, local, where_ref, lengths_ref, *refs
):
    gathered = refs[:pieces]
    caps_ref, cot_ref, qkv_ref, outw_ref, gains_ref = refs[pieces : pieces + 5]
    out_ref, grad_ref, gain_ref = refs[pieces + 5 : pieces + 8]
    part_refs = refs[pieces + 8 : pieces + 8 + pieces]
    keep_ref, send_ref, acc = refs[pieces + 8 + pieces :]
    width = caps_ref.shape[1]
    slots = gathered[0].shape[0]
    count = caps_ref.shape[0]
    keys_n = pieces * slots
    runs = lengths_ref.shape[1]

    token = lax.broadcasted_iota(jnp.int32, (count, keys_n), 0)
    key = lax.broadcasted_iota(jnp.int32, (count, keys_n), 1)
    slot = key % slots
    group = token // local
    position = token - group * local + where_ref[0] * local
    document = jnp.zeros((count, keys_n), jnp.int32)
    for m in range(groups):
        end = jnp.int32(0)
        for j in range(runs):
            end = end + lengths_ref[m, j]
            document = document + jnp.where((group == m) & (position >= end), 1, 0)
    allowed = slot == group * clips + document % clips
    valid = (document[:, 0:1] < runs - 1).astype(f32)

    pack = caps_ref[...].astype(f32)
    unit, inv = unit_norm(pack)
    gain = gains_ref[3:4, :]
    normed = (unit * gain).astype(bf16)
    visual = jnp.concatenate([g[...] for g in gathered], axis=0)
    queries = nn(normed, qkv_ref[0, 0]).astype(bf16)
    keys = nn(visual, qkv_ref[0, 1]).astype(bf16)
    values = nn(visual, qkv_ref[0, 2]).astype(bf16)

    masks = [head_mask((count, width), 1, h) for h in range(HEADS)]
    zero = jnp.zeros((count, width), bf16)

    def by_head(x):
        return jnp.concatenate([jnp.where(m, x, zero) for m in masks], axis=0)

    def merge(x):
        cut = [x[h * count : (h + 1) * count] for h in range(HEADS)]
        return functools.reduce(jnp.add, [jnp.where(m, c, 0.0) for m, c in zip(masks, cut)])

    allowed_all = jnp.concatenate([allowed.astype(jnp.int32)] * HEADS, axis=0) > 0
    split_q = by_head(queries)
    scores = jnp.where(allowed_all, nt(split_q, keys) * SCALE, MASKED)
    expo = jnp.exp(scores - jnp.max(scores, axis=1, keepdims=True))
    probs = expo / jnp.sum(expo, axis=1, keepdims=True)
    low = probs.astype(bf16)
    context = merge(nn(low, values)).astype(bf16)
    out_ref[...] = (pack + valid * nn(context, outw_ref[0])).astype(bf16)

    cot = cot_ref[...].astype(f32)
    branch = (cot * valid).astype(bf16)
    split_d = by_head(nt(branch, outw_ref[0]).astype(bf16))
    dvalues = tn(low, split_d)
    dprobs = nt(split_d, values)
    dscores = probs * (dprobs - jnp.sum(dprobs * probs, axis=1, keepdims=True))
    dscores = jnp.where(allowed_all, dscores, 0.0).astype(bf16)
    dqueries = (merge(nn(dscores, keys)) * SCALE).astype(bf16)
    dkeys = tn(dscores, split_q) * SCALE
    dnormed = nt(dqueries, qkv_ref[0, 0])
    grad_ref[...] = (cot + norm_back(unit, inv, gain, dnormed)).astype(bf16)
    gain_ref[...] = jnp.concatenate([row_sum(dnormed * unit), jnp.zeros((7, width), f32)], axis=0)
    low_k, low_v = dkeys.astype(bf16), dvalues.astype(bf16)
    part = nt(low_k, qkv_ref[0, 1]) + nt(low_v, qkv_ref[0, 2])
    for g in range(pieces):
        part_refs[g][...] = part[g * slots : (g + 1) * slots]
    if acc.shape[0] > 4 * width:
        acc[...] = jnp.zeros(acc.shape, f32)
    acc[0:width, :] = tn(normed, dqueries)
    acc[width : 2 * width, :] = tn(visual, low_k)
    acc[2 * width : 3 * width, :] = tn(visual, low_v)
    acc[3 * width : 4 * width, :] = tn(context, branch)
    emit(where_ref, acc, keep_ref, send_ref)


def captions_step(where, lengths, gathered, caps, cot, qkv, outw, gains, plan):
    count, width = caps.shape
    groups = lengths.shape[0]
    pieces = len(gathered)
    slots = gathered[0].shape[0]
    operands = list(gathered) + [caps, cot, qkv, outw, gains]
    acc_rows, packet_specs, packet_shapes = plan.packet(4 * width, width)
    return pl.pallas_call(
        functools.partial(caption_kernel, pieces, groups, plan.clips, count // groups),
        grid=(1,),
        in_specs=[scalars(), scalars()]
        + [full(x.shape) for x in operands[:-3]]
        + [
            pl.BlockSpec((1, 3, width, width), lambda i: (2, 0, 0, 0)),
            pl.BlockSpec((1, width, width), lambda i: (2, 0, 0)),
            full(gains.shape),
        ],
        out_specs=[full((count, width))] * 2
        + [full((8, width))]
        + [full((slots, width))] * pieces
        + packet_specs,
        out_shape=[shape_of((count, width), bf16)] * 2
        + [shape_of((8, width), f32)]
        + [shape_of((slots, width), f32)] * pieces
        + packet_shapes,
        scratch_shapes=[pltpu.VMEM((acc_rows, width), f32)],
        compiler_params=params(12),
        cost_estimate=cost(4e9, 8e6),
        name="captions_step",
    )(where, lengths, *operands)


def mlp_kernel(
    pieces, patch, ff, where_ref, resid_ref, cot_ref, final_ref, gains_ref, up_ref, down_ref, *refs
):
    parts = refs[:pieces]
    out_ref, dresid_ref, gain_ref, keep_ref, send_ref, acc, dcls = refs[-7:]
    step = pl.program_id(0)
    batch, rows, width = resid_ref.shape
    wide = acc.shape[1]
    blocks = ff // wide

    @pl.when(step == 0)
    def _():
        acc[...] = jnp.zeros(acc.shape, f32)
        dvisual = functools.reduce(jnp.add, [p[...] for p in parts])
        unit, inv = unit_norm(final_ref[...])
        dcls[...] = norm_back(unit, inv, gains_ref[2:3, :], dvisual)
        gain_ref[...] = jnp.concatenate(
            [jnp.zeros((1, width), f32), row_sum(dvisual * unit), jnp.zeros((6, width), f32)],
            axis=0,
        )

    resid = resid_ref[...].reshape(batch * rows, width)
    gain = gains_ref[1:2, :]
    unit, inv = unit_norm(resid)
    normed32 = unit * gain
    normed = normed32.astype(bf16)
    normed_t = normed32.T.astype(bf16)
    pieces_d = []
    for i in range(batch):
        one = pad_rows(cot_ref[i].astype(f32), rows)
        pieces_d.append(put_row(one, 0, one[0:1] + dcls[pl.ds(step * batch + i, 1), :]))
    dfinal = jnp.concatenate(pieces_d, axis=0)
    branch = dfinal.astype(bf16)
    branch_t = dfinal.T.astype(bf16)
    final = resid
    dnormed = jnp.zeros((batch * rows, width), f32)
    for c in range(blocks):
        span = slice(c * wide, (c + 1) * wide)
        hidden = nn(normed, up_ref[:, span])
        gate = sigmoid(1.702 * hidden)
        active = (hidden * gate).astype(bf16)
        final = final + nn(active, down_ref[span, :])
        dactive = nt(branch, down_ref[span, :])
        dhidden = (dactive * gate * (1.0 + 1.702 * hidden * (1.0 - gate))).astype(bf16)
        dnormed = dnormed + nt(dhidden, up_ref[:, span])
        acc[c * width : (c + 1) * width, :] += nn(normed_t, dhidden)
        acc[(blocks + c) * width : (blocks + c + 1) * width, :] += nn(branch_t, active)
    for i in range(batch):
        out_ref[i] = final[i * rows : i * rows + patch].astype(bf16)
    dresid = dfinal + norm_back(unit, inv, gain, dnormed)
    dresid_ref[...] = dresid.reshape(batch, rows, width)
    gain_ref[0:1, :] += row_sum(dnormed * unit)

    @pl.when(step == pl.num_programs(0) - 1)
    def _():
        emit(where_ref, acc, keep_ref, send_ref)


def mlp_step(where, resid, cot, final, gains, up, down, parts, plan, after=()):
    count, rows, width = resid.shape
    patch = cot.shape[1]
    ff = up.shape[1]
    slots = final.shape[0]
    batch = share_of(count, 2)
    wide = 2 * width
    acc_rows, packet_specs, packet_shapes = plan.packet(2 * ff * width // wide, wide)
    return pl.pallas_call(
        functools.partial(mlp_kernel, len(parts), patch, ff),
        grid=(count // batch,),
        in_specs=[
            scalars(),
            frames_block(batch, (rows, width)),
            frames_block(batch, (patch, width)),
            full((slots, width)),
            full(gains.shape),
            full(up.shape),
            full(down.shape),
        ]
        + [full((slots, width))] * len(parts)
        + [pl.BlockSpec(memory_space=pl.ANY)] * len(after),
        out_specs=[
            frames_block(batch, (patch, width)),
            frames_block(batch, (rows, width)),
            full((8, width)),
        ]
        + packet_specs,
        out_shape=[
            shape_of((count, patch, width), bf16),
            shape_of((count, rows, width), f32),
            shape_of((8, width), f32),
        ]
        + packet_shapes,
        scratch_shapes=[pltpu.VMEM((acc_rows, wide), f32), pltpu.VMEM((slots, width), f32)],
        compiler_params=params(36),
        cost_estimate=cost(20e9, 20e6),
        name="mlp_step",
    )(where, resid, cot, final, gains, up, down, *parts, *after)


def attend_back_kernel(tokens, first, last, waits, where_ref, normed_ref, kv_ref, *refs):
    (
        video_ref, message_ref, nmsg_ref, kvmsg_ref, ctx_ref, lse_ref, dresid_ref, gains_ref,
        wq_ref, wk_ref, wv_ref, wo_ref,
    ) = refs[:12]
    refs = refs[12:]
    if first:
        carried, refs = refs[1:5], refs[5:]
    refs = refs[waits:]
    outs = refs[: 6 if last else 5]
    grad_ref, dmsg_ref, dcls_ref, gain_ref = outs[:4]
    acc, wqt, wkt, wall = refs[len(outs) :]
    here = pl.program_id(0)
    step = here + first
    batch, rows, width = dresid_ref.shape
    patch = tokens - 1

    @pl.when(here == 0)
    def _():
        wqt[...] = wq_ref[...].T
        wkt[...] = wk_ref[...].T
        wall[:, 0:width] = wq_ref[...]
        wall[:, width : 2 * width] = wk_ref[...]
        wall[:, 2 * width : 3 * width] = wv_ref[...]
        for k, ref in enumerate((dmsg_ref, dcls_ref, gain_ref, acc)):
            ref[...] = carried[k][...] if first else jnp.zeros(ref.shape, f32)

    frames = range(batch)
    normed, kv = [], []
    for i in frames:
        normed.append(with_message(normed_ref[i], nmsg_ref, tokens, step * batch + i))
        kv.append(with_message(kv_ref[i], kvmsg_ref, tokens, step * batch + i))
    branch = [dresid_ref[i].astype(bf16) for i in frames]
    queries_t = [nt(wqt[...], n).astype(bf16) * jnp.bfloat16(SCALE) for n in normed]
    dcontext_t = [nt(wo_ref[...], b).astype(bf16) for b in branch]
    keys_t = [nt(wkt[...], n).astype(bf16) for n in normed]
    acc[3 * width : 4 * width, :] += functools.reduce(
        jnp.add, [nn(ctx_ref[i], branch[i]) for i in frames]
    )
    jobs = [(i, h) for i in frames for h in range(HEADS)]
    own = [slice(h * HEAD_DIM, (h + 1) * HEAD_DIM) for h in range(HEADS)]
    scores, dprobs, low, dscores, dq, dk, dv = {}, {}, {}, {}, {}, {}, {}

    def score(job):
        i, h = job
        scores[job] = nn(pair_lanes(kv[i], h), half_pair(queries_t[i], h))
        dprobs[job] = nn(pair_lanes(kv[i], HEADS + h), half_pair(dcontext_t[i], h))

    def soften(job):
        i, h = job
        probs = jnp.exp(masked_tail(scores.pop(job), tokens) - lse_ref[i, h : h + 1, :])
        low[job] = probs.astype(bf16)
        weighted = dprobs.pop(job) * probs
        dscores[job] = (weighted - probs * row_sum(weighted)).astype(bf16)

    def mix(job):
        i, h = job
        dq[job] = nn(keys_t[i][own[h]], dscores[job]) * SCALE
        dk[job] = nt(queries_t[i][own[h]], dscores.pop(job))
        dv[job] = nt(dcontext_t[i][own[h]], low.pop(job))

    stagger(jobs, [score, soften, mix], 2)
    dall = []
    for i in frames:
        parts = [d[i, h] for d in (dq, dk, dv) for h in range(HEADS)]
        dall.append(jnp.concatenate(parts, axis=0).astype(bf16))
    acc[0 : 3 * width, :] += functools.reduce(
        jnp.add, [nn(dall[i], normed[i]) for i in frames]
    )
    gain_sum = jnp.zeros((1, width), f32)
    for i in frames:
        dnormed = nn(wall[...], dall[i]).T
        at = pl.ds(step * batch + i, 1)
        base = put_row(pad_rows(video_ref[i].astype(f32), rows), tokens - 1, message_ref[at, :])
        unit, inv = unit_norm(base)
        dtokens = dresid_ref[i] + norm_back(unit, inv, gains_ref[0:1, :], dnormed)
        gain_sum = gain_sum + row_sum(dnormed * unit)
        grad_ref[i] = dtokens[:patch].astype(bf16)
        dcls_ref[at, :] = dtokens[0:1]
        dmsg_ref[at, :] = dtokens[patch : patch + 1]
    gain_ref[0:1, :] += gain_sum

    @pl.when(here == pl.num_programs(0) - 1)
    def _():
        if last:
            emit(where_ref, acc, *outs[4:])
        else:
            outs[4][...] = acc[...]


def attend_back(
    where, normed, kv, video, message, nmsg, kvmsg, ctx, lse, dresid, gains, qkv, outw, plan,
    batch, first, steps, carried=(), after=(),
):
    count, rows, width = normed.shape
    patch = video.shape[1]
    slots = message.shape[0]
    last = (first + steps) * batch == count
    acc_rows, packet_specs, packet_shapes = plan.packet(4 * width, width)
    if not last:
        packet_specs, packet_shapes = [full((acc_rows, width))], [shape_of((acc_rows, width), f32)]

    def block(shape):
        return pl.BlockSpec((batch,) + shape, lambda i, *_: (i + first, 0, 0))

    anywhere = pl.BlockSpec(memory_space=pl.ANY)
    carry_specs = [anywhere] + [full(x.shape) for x in carried[1:]] if carried else []
    return pl.pallas_call(
        functools.partial(attend_back_kernel, patch + 1, first, last, len(after)),
        grid=(steps,),
        in_specs=[
            scalars(),
            block((rows, width)),
            block((rows, 2 * width)),
            block((patch, width)),
            full((slots, width)),
            full((slots, width)),
            full((slots, 2 * width)),
            block((width, rows)),
            block((8, rows)),
            block((rows, width)),
            full(gains.shape),
            square(width, 1, 0),
            square(width, 1, 1),
            square(width, 1, 2),
            square(width, 1),
        ]
        + carry_specs
        + [anywhere] * len(after),
        out_specs=[block((patch, width))]
        + [full((slots, width))] * 2
        + [full((8, width))]
        + packet_specs,
        out_shape=[shape_of((count, patch, width), bf16)]
        + [shape_of((slots, width), f32)] * 2
        + [shape_of((8, width), f32)]
        + packet_shapes,
        input_output_aliases={15: 0} if carried else {},
        scratch_shapes=[
            pltpu.VMEM((acc_rows, width), f32),
            pltpu.VMEM((width, width), bf16),
            pltpu.VMEM((width, width), bf16),
            pltpu.VMEM((width, 3 * width), bf16),
        ],
        compiler_params=params(26),
        cost_estimate=cost(4.5e9 * steps, 4e6 * steps),
        name="attend_back",
    )(
        where, normed, kv, video, message, nmsg, kvmsg, ctx, lse, dresid, gains, qkv, qkv, qkv,
        outw, *carried, *after,
    )


class Groups:
    def __init__(self, layout, slots):
        self.segs, self.frames, self.clips = layout
        self.slots = slots
        self.groups = self.segs * self.clips
        self.together = max(1, min(self.groups, 512 // (self.frames * slots)))
        self.steps = self.groups // self.together
        self.rows = self.frames * self.together * slots
        per_group = self.frames * slots
        self.side = per_group * max(1, min(self.together, 128 // per_group))
        self.blocks = [slice(at, at + self.side) for at in range(0, self.rows, self.side)]
        self.jobs = [(i, h) for i in range(len(self.blocks)) for h in range(HEADS)]

    def row_of(self, s, f, c):
        group = s * self.clips + c
        step, inside = group // self.together, group % self.together
        return step, pl.multiple_of((inside * self.frames + f) * self.slots, 16)

    def every(self, where_ref):
        me_f, me_s, me_c = where_ref[0], where_ref[1], where_ref[2]
        for a in range(self.segs):
            for b in range(self.frames):
                for d in range(self.clips):
                    yield a, b, d, *self.row_of(me_s ^ a, me_f ^ b, me_c ^ d)

    def run(self, batch):
        def first(ref, at, value):
            ref[at] = value

        def again(ref, at, value):
            ref[at] += value

        batch(0, first)
        if self.steps > 1:
            pl.loop(1, self.steps)(lambda step: batch(step, again))


def join(groups, *parts):
    lanes = [
        jnp.concatenate([p[i, h] for p in parts for h in range(HEADS)], axis=0)
        for i in range(len(groups.blocks))
    ]
    return (jnp.concatenate(lanes, axis=1) if len(lanes) > 1 else lanes[0]).astype(bf16)


OWN = [slice(h * HEAD_DIM, (h + 1) * HEAD_DIM) for h in range(HEADS)]


def message_forward_kernel(groups, where_ref, *refs):
    side = refs[: groups.segs]
    (
        mw_ref, mg_ref, qkv_ref, classes_ref, start_ref, values_ref, qt_ref, kt_ref, probs_ref,
        ctx_ref, wqt, wkt, wvt,
    ) = refs[groups.segs :]
    for a, b, d, step, row in groups.every(where_ref):
        classes_ref[step, pl.ds(row, groups.slots), :] = side[a][d, b]
    wqt[...] = qkv_ref[0, 0].T
    wkt[...] = qkv_ref[0, 1].T
    wvt[...] = qkv_ref[0, 2].T
    edge = (groups.side, groups.side)
    key, query = lax.broadcasted_iota(jnp.int32, edge, 0), lax.broadcasted_iota(jnp.int32, edge, 1)
    per_group = groups.frames * groups.slots
    same = (key % groups.slots == query % groups.slots) & (key // per_group == query // per_group)

    def batch(step, put):
        del put
        start = nn(classes_ref[step], mw_ref[...]).astype(bf16)
        start_ref[step] = start
        unit, _ = unit_norm(start.astype(f32))
        normed = (unit * mg_ref[...]).astype(bf16)
        keys = nn(normed, qkv_ref[0, 1]).astype(bf16)
        values_ref[step] = nn(normed, qkv_ref[0, 2]).astype(bf16)
        queries_t = nt(wqt[...], normed).astype(bf16) * jnp.bfloat16(SCALE)
        values_t = nt(wvt[...], normed).astype(bf16)
        qt_ref[step] = queries_t
        kt_ref[step] = nt(wkt[...], normed).astype(bf16)
        scores, low, ctx = {}, {}, {}

        def score(job):
            i, h = job
            at = groups.blocks[i]
            scores[job] = nn(pair_lanes(keys[at], h), half_pair(queries_t[:, at], h))

        def soften(job):
            i, h = job
            one = jnp.where(same, scores.pop(job), MASKED)
            expo = jnp.exp(one - jnp.max(one, axis=0, keepdims=True))
            probs = expo * (1.0 / row_sum(expo))
            probs_ref[step, i * HEADS + h] = probs.astype(probs_ref.dtype)
            low[job] = probs.astype(bf16)

        def mix(job):
            i, h = job
            ctx[job] = nn(values_t[OWN[h], groups.blocks[i]], low.pop(job))

        stagger(groups.jobs, [score, soften, mix], 3)
        ctx_ref[step] = join(groups, ctx)

    groups.run(batch)


def message_forward(where, side, mw, mg, qkv, groups):
    width = mw.shape[0]
    rows, steps = groups.rows, groups.steps
    outs = [
        shape_of((steps, rows, width), bf16),
        shape_of((steps, rows, width), bf16),
        shape_of((steps, rows, width), bf16),
        shape_of((steps, width, rows), bf16),
        shape_of((steps, width, rows), bf16),
        shape_of((steps, len(groups.jobs), groups.side, groups.side), f32 if steps == 1 else bf16),
        shape_of((steps, width, rows), bf16),
    ]
    return pl.pallas_call(
        functools.partial(message_forward_kernel, groups),
        grid=(1,),
        in_specs=[scalars()]
        + [full(x.shape) for x in side]
        + [
            full(mw.shape),
            full(mg.shape),
            pl.BlockSpec((1, 3, width, width), lambda i: (0, 0, 0, 0)),
        ],
        out_specs=[full(x.shape) for x in outs],
        out_shape=outs,
        scratch_shapes=[pltpu.VMEM((width, width), bf16)] * 3,
        compiler_params=params(56),
        cost_estimate=cost(3e9, 6e6),
        name="message_forward",
    )(where, *side, mw, mg, qkv)


def message_back_kernel(layout, groups, where_ref, *refs):
    frame_part(layout, where_ref, *refs)
    message_part(groups, where_ref, *refs)


def frame_part(layout, where_ref, *refs):
    segs, frames, clips = layout
    pieces, refs = refs[: segs * frames], refs[segs * frames + 7 :]
    big_ref, out_ref, whole = refs[6], refs[7], refs[12]
    width = out_ref.shape[-1]
    chunk = whole.shape[0] // (segs * frames * clips)
    place(
        layout,
        where_ref,
        lambda a, b, d: pieces[a * frames + b][d * chunk : (d + 1) * chunk, :],
        whole,
        chunk,
    )
    for j in range(3):
        big_ref[1, j] = whole[j * width : (j + 1) * width, :].astype(f32).T
    out_ref[1] = whole[3 * width : 4 * width, :].astype(f32)


def message_part(groups, where_ref, *refs):
    count = groups.segs * groups.frames
    pieces, refs = refs[:count], refs[count:]
    classes_ref, start_ref, values_ref, qt_ref, kt_ref, probs_ref, ctx_ref = refs[:7]
    mw_ref, mg_ref, qkv_ref, outw_ref = refs[7:11]
    big_ref, out_ref, mwg_ref, gain_ref, gains_ref, dclass_ref, _, dmsgs, dstart, wall = refs[13:]
    width, slots = mw_ref.shape[0], groups.slots
    for a, b, d, step, row in groups.every(where_ref):
        piece = pieces[a * groups.frames + b]
        at = piece.shape[0] - (groups.clips - d) * slots
        dmsgs[step, pl.ds(row, slots), :] = piece[at : at + slots, :]
    gain_total = jnp.zeros((slots, width), f32)
    for i in range(groups.frames * groups.together):
        for step in range(groups.steps):
            gain_total += dmsgs[step, i * slots : (i + 1) * slots, :].astype(f32)
    gains_ref[...] = gain_total[slots - 4 : slots]
    for j in range(3):
        wall[:, j * width : (j + 1) * width] = qkv_ref[0, j]
    index = lax.broadcasted_iota(jnp.int32, (groups.rows, 1), 0) % slots
    my_step, my_row = groups.row_of(where_ref[1], where_ref[0], where_ref[2])

    def batch(step, put):
        dm = jnp.where(index < slots - 6, dmsgs[step].astype(f32), 0.0).astype(bf16)
        unit, inv = unit_norm(start_ref[step].astype(f32))
        normed = (unit * mg_ref[...]).astype(bf16)
        dcontext_t = nt(outw_ref[0], dm).astype(bf16)
        values, queries_t, keys_t = values_ref[step], qt_ref[step], kt_ref[step]
        dprobs, low, dscores, dq, dk, dv = {}, {}, {}, {}, {}, {}

        def score(job):
            i, h = job
            at = groups.blocks[i]
            dprobs[job] = nn(pair_lanes(values[at], h), half_pair(dcontext_t[:, at], h))

        def soften(job):
            i, h = job
            probs = probs_ref[step, i * HEADS + h].astype(f32)
            low[job] = probs.astype(bf16)
            weighted = dprobs.pop(job) * probs
            dscores[job] = (weighted - probs * row_sum(weighted)).astype(bf16)

        def mix(job):
            i, h = job
            at = groups.blocks[i]
            dq[job] = nn(keys_t[OWN[h], at], dscores[job]) * SCALE
            dk[job] = nt(queries_t[OWN[h], at], dscores.pop(job))
            dv[job] = nt(dcontext_t[OWN[h], at], low.pop(job))

        stagger(groups.jobs, [score, soften, mix], 2)
        put(out_ref, 0, nn(ctx_ref[step], dm))
        dall = join(groups, dq, dk, dv)
        grads = nn(dall, normed)
        for j in range(3):
            put(big_ref, (0, j), grads[j * width : (j + 1) * width].T)
        dnormed = nn(wall[...], dall).T
        put(gain_ref, ..., jnp.sum(dnormed * unit, axis=0))
        ds = norm_back(unit, inv, mg_ref[...], dnormed) + dm.astype(f32)
        dstart[...] = ds
        put(mwg_ref, ..., tn(classes_ref[step], ds.astype(bf16)))

        @pl.when(my_step == step)
        def _():
            dclass_ref[...] = nt(dstart[pl.ds(my_row, slots), :].astype(bf16), mw_ref[...])

    groups.run(batch)


def message_back(where, pieces, forward, mw, mg, qkv, outw, big, out, layout, groups):
    width = mw.shape[0]
    operands = list(pieces) + list(forward) + [mw, mg]
    chunk = pieces[0].shape[0] // groups.clips - groups.slots
    return pl.pallas_call(
        functools.partial(message_back_kernel, layout, groups),
        grid=(1,),
        in_specs=[scalars()]
        + [full(x.shape) for x in operands]
        + [
            pl.BlockSpec((1, 3, width, width), lambda i: (0, 0, 0, 0)),
            pl.BlockSpec((1, width, width), lambda i: (0, 0, 0)),
            pl.BlockSpec(memory_space=pl.ANY),
            pl.BlockSpec(memory_space=pl.ANY),
        ],
        out_specs=[
            pl.BlockSpec((2, 3, width, width), lambda i: (0, 0, 0, 0)),
            pl.BlockSpec((2, width, width), lambda i: (0, 0, 0)),
            full((width, width)),
            full((width,)),
            full((4, width)),
            full((groups.slots, width)),
        ],
        out_shape=[
            shape_of((3, 3, width, width), f32),
            shape_of((3, width, width), f32),
            shape_of((width, width), f32),
            shape_of((width,), f32),
            shape_of((4, width), f32),
            shape_of((groups.slots, width), f32),
        ],
        input_output_aliases={len(operands) + 3: 0, len(operands) + 4: 1},
        scratch_shapes=[
            pltpu.VMEM((groups.groups * groups.frames * chunk, width), bf16),
            pltpu.VMEM((groups.steps, groups.rows, width), bf16),
            pltpu.VMEM((groups.rows, width), f32),
            pltpu.VMEM((width, 3 * width), bf16),
        ],
        compiler_params=params(30 if groups.steps == 1 else 60),
        cost_estimate=cost(4e9, 12e6),
        name="message_back",
    )(where, *operands, qkv, outw, big, out)


def emit(where_ref, acc, keep_ref, send_ref):
    frames, clips, chunk = keep_ref.shape[:3]
    me_f, me_s = where_ref[0], where_ref[1]
    for a, out in enumerate((keep_ref, send_ref)):
        for b in range(frames):
            for d in range(clips):
                to = ((me_s ^ a) * frames + (me_f ^ b)) * clips + d
                at = pl.multiple_of(to * chunk, 16)
                out[b, d] = acc[pl.ds(at, chunk), :].astype(bf16)


class Plan:
    def __init__(self, clips):
        self.clips = clips
        self.segs = lax.axis_size("seg")
        self.frames = lax.axis_size("frame")
        self.rings = lax.axis_size("clip")
        self.layout = (self.segs, self.frames, self.rings)
        self.devices = self.segs * self.frames * self.rings

    def chunk(self, rows):
        share = -(-rows // self.devices)
        return -(-share // 16) * 16

    def packet(self, rows, width):
        chunk = self.chunk(rows)
        shape = (self.frames, self.rings, chunk, width)
        return chunk * self.devices, [full(shape)] * 2, [shape_of(shape, bf16)] * 2


def swap(x, axis, k):
    count = lax.axis_size(axis)
    return lax.ppermute(x, axis, [(i, i ^ k) for i in range(count)])


def behind(x, *others):
    return lax.optimization_barrier((x, others))[0]


class Sum:
    def __init__(self, arrays, views=None):
        self.arrays = list(arrays)
        self.views = list(views or [()] * len(self.arrays))

    def part(self, view):
        return Sum(self.arrays, [v + (view,) for v in self.views])

    def plus(self, *arrays):
        return Sum(self.arrays + list(arrays), self.views + [()] * len(arrays))

    def value(self):
        terms = []
        for x, views in zip(self.arrays, self.views):
            for view in views:
                x = view(x)
            terms.append(x.astype(f32))
        return functools.reduce(jnp.add, terms).astype(bf16)


jax.tree_util.register_pytree_node(
    Sum, lambda s: (s.arrays, s.views), lambda views, arrays: Sum(arrays, views)
)


def at(k):
    return lambda x: x[k]


def total(one, two):
    return (one.astype(f32) + two.astype(f32)).astype(bf16)


def reduce_seg(keep, send):
    return Sum([keep, swap(send, "seg", 1)])


def frame_sends(terms):
    return [terms.part(at(b)).value() for b in range(1, lax.axis_size("frame"))]


def reduce_frame(terms, sends):
    return terms.part(at(0)).plus(*[swap(x, "frame", b + 1) for b, x in enumerate(sends)])


def clip_bits():
    count = lax.axis_size("clip")
    return [1 << j for j in range(count.bit_length() - 1)]


def swap_two(one, two, axis, k):
    width = one.shape[-1]
    rows = one.size // width
    got = swap(jnp.concatenate([one.reshape(-1, width), two.reshape(-1, width)]), axis, k)
    return got[:rows].reshape(one.shape), got[rows:].reshape(two.shape)


def exchange(part, rows, bit):
    got, got_rows = swap_two(part, rows, "clip", bit)
    return total(part, got), jnp.concatenate([rows, got_rows])


def gather_frame(held):
    return [held] + [swap(held, "frame", b) for b in range(1, lax.axis_size("frame"))]


def gather_seg(held):
    return held + [swap(h, "seg", 1) for h in held]


def place(layout, where_ref, piece, whole, chunk):
    segs, frames, clips = layout
    me_f, me_s = where_ref[0], where_ref[1]
    for a in range(segs):
        for b in range(frames):
            for d in range(clips):
                of = ((me_s ^ a) * frames + (me_f ^ b)) * clips + d
                whole[pl.ds(pl.multiple_of(of * chunk, 16), chunk), :] = piece(a, b, d)


def unpack_kernel(layout, where_ref, *refs):
    segs, frames, clips = layout
    main = refs[:segs]
    up_ref, down_ref, whole = refs[segs:]
    width, ff = up_ref.shape
    wide = whole.shape[1]
    place(layout, where_ref, lambda a, b, d: main[a][b * clips + d], whole, main[0].shape[1])
    blocks = ff // wide
    for c in range(blocks):
        span = slice(c * wide, (c + 1) * wide)
        up_ref[:, span] = whole[c * width : (c + 1) * width, :].astype(f32)
        other = whole[(blocks + c) * width : (blocks + c + 1) * width, :]
        down_ref[span, :] = other.astype(f32).T


def unpack(where, main, width, ff, plan):
    chunk, wide = main[0].shape[1:]
    return pl.pallas_call(
        functools.partial(unpack_kernel, plan.layout),
        grid=(1,),
        in_specs=[scalars()] + [full(x.shape) for x in main],
        out_specs=[full((width, ff)), full((ff, width))],
        out_shape=[shape_of((width, ff), f32), shape_of((ff, width), f32)],
        scratch_shapes=[pltpu.VMEM((plan.devices * chunk, wide), bf16)],
        compiler_params=params(40),
        cost_estimate=cost(2e9, 10e6),
        name="unpack",
    )(where, *main)


def unpack_side_kernel(layout, where_ref, *refs):
    segs = layout[0]
    side = refs[:segs]
    big_ref, out_ref, whole = refs[segs:]
    width = out_ref.shape[-1]
    place(layout, where_ref, lambda a, b, d: side[a][b, d], whole, side[0].shape[2])
    for j in range(3):
        big_ref[0, j] = whole[j * width : (j + 1) * width, :].astype(f32)
    out_ref[0] = whole[3 * width : 4 * width, :].astype(f32)


def unpack_side(where, side, plan):
    rows, width = side[0].shape[2:]
    return pl.pallas_call(
        functools.partial(unpack_side_kernel, plan.layout),
        grid=(1,),
        in_specs=[scalars()] + [full(x.shape) for x in side],
        out_specs=[
            pl.BlockSpec((1, 3, width, width), lambda i: (2, 0, 0, 0)),
            pl.BlockSpec((1, width, width), lambda i: (2, 0, 0)),
        ],
        out_shape=[shape_of((3, 3, width, width), f32), shape_of((3, width, width), f32)],
        scratch_shapes=[pltpu.VMEM((plan.devices * rows, width), bf16)],
        compiler_params=params(30),
        cost_estimate=cost(1e9, 4e6),
        name="unpack_side",
    )(where, *side)


def last_rows_kernel(gain_a, gain_b, gain_c, dmsg_ref, out_ref):
    slots, width = dmsg_ref.shape
    rows = [
        dmsg_ref[0 : slots - 6, :],
        jnp.zeros((2, width), f32),
        gain_a[0:1, :],
        gain_b[0:1, :],
        gain_b[1:2, :],
        gain_c[0:1, :],
    ]
    out_ref[...] = jnp.concatenate(rows, axis=0).astype(bf16)


def last_rows(gain_a, gain_b, gain_c, dmsg):
    return pl.pallas_call(
        last_rows_kernel,
        out_shape=shape_of(dmsg.shape, bf16),
        name="last_rows",
    )(gain_a, gain_b, gain_c, dmsg)


def local(
    video, captions, caption_lengths, message_weight, message_gain, qkv_weights, out_weights,
    mlp_up, mlp_down, gains, video_cot, caption_cot,
):
    micro, clips, per_frame, patch, width = video.shape
    count = micro * clips * per_frame
    ff = mlp_up.shape[1]
    plan = Plan(clips)
    tokens = patch + 1
    rows = -(-tokens // 16) * 16
    slots = -(-(count + 6) // 16) * 16
    where = jnp.stack(
        [lax.axis_index("frame"), lax.axis_index("seg"), lax.axis_index("clip")]
    ).astype(jnp.int32)
    frames = video.reshape(count, patch, width)
    cots = video_cot.reshape(count, patch, width)
    caps = captions.reshape(-1, width)
    cap_cots = caption_cot.reshape(-1, width)
    lengths = caption_lengths.reshape(micro, -1)
    gain = message_gain.reshape(1, width)

    classes = class_rows(video, slots)
    gathered = gather_frame(classes)
    normed, kv = norm_tokens(frames, gains, qkv_weights, rows)
    message, nmsg, kvmsg, visual, final = first_rows(
        gathered, message_weight, gain, qkv_weights, out_weights, mlp_up, mlp_down, gains,
        kv, tokens,
    )
    visuals = gather_frame(visual)
    results = captions_step(
        where, lengths, visuals, caps, cap_cots, qkv_weights, out_weights, gains, plan
    )
    caption_out, caption_grad, gain_c = results[:3]
    parts = list(results[3:-2])
    parts = [parts[0]] + [swap(parts[b], "frame", b) for b in range(1, plan.frames)]
    bits = clip_bits()
    rows_all = jnp.stack(gathered)[None]
    side = reduce_seg(*results[-2:])
    side = behind(side, results[3])
    sends = frame_sends(side)
    resid, ctx, lse = attend(
        normed, kv, frames, message, nmsg, kvmsg, qkv_weights, out_weights, tokens, sends
    )
    side = reduce_frame(side, sends)
    parts, resid, side = behind((parts, resid, side))
    side = side.value()
    side, resid = behind((side, resid))
    video_out, dresid, gain_b, keep, send = mlp_step(
        where, resid, cots, final, gains, mlp_up, mlp_down, parts, plan
    )
    for bit in bits[:-1]:
        side, rows_all = exchange(side, rows_all, bit)
    side, rows_all, video_out, dresid, keep, send = behind(
        (side, rows_all, video_out, dresid, keep, send)
    )
    main = reduce_seg(keep, send)
    turned = video_out.reshape(video.shape).transpose(1, 2, 3, 0, 4)
    main, dresid, turned = behind((main, dresid, turned))
    video_out = turned.transpose(3, 0, 1, 2, 4)
    sends = frame_sends(main)
    sends, dresid, side, rows_all = behind((sends, dresid, side, rows_all))
    batch = share_of(count, 2)
    steps = count // batch
    late_steps = 2
    back = functools.partial(
        attend_back, where, normed, kv, frames, message, nmsg, kvmsg, ctx, lse, dresid, gains,
        qkv_weights, out_weights, plan, batch,
    )
    carried = back(0, steps - late_steps)
    main = reduce_frame(main, sends)
    side, rows_all = exchange(side, rows_all, bits[-1])
    carried, main, side, rows_all = behind((carried, main, side, rows_all))
    main = main.value()
    main, carried, side = behind((main, carried, side))
    for bit in bits[:-1]:
        main = total(main, swap(main, "clip", bit))
    side = gather_frame(side)
    grad, dmsg, dcls, gain_a, keep, send = back(steps - late_steps, late_steps, carried)
    main, side, keep, send, gain_a, dmsg = behind((main, side, keep, send, gain_a, dmsg))

    main = total(main, swap(main, "clip", bits[-1]))
    late = reduce_seg(keep, send)
    rest = last_rows(gain_a, gain_b, gain_c, dmsg)
    side = jnp.stack(side)
    other, other_rows = swap_two(side, rows_all, "seg", 1)
    late, rest = behind((late, rest))
    late = reduce_frame(late, frame_sends(late))
    main, late, other, other_rows = behind((main, late, other, other_rows))

    held = gather_frame(main)
    late, rest = late.value(), rest[None]
    for bit in bits:
        late, rest = exchange(late, rest, bit)
    big, out = unpack_side(where, [side, other], plan)
    groups = Groups(plan.layout, slots)
    forward = message_forward(
        where, [rows_all, other_rows], message_weight, gain, qkv_weights, groups
    )
    held, late, rest, big, forward = behind((held, late, rest, big, forward))

    late = gather_frame(jnp.concatenate([late.reshape(-1, width), rest.reshape(-1, width)]))
    held = gather_seg([jnp.concatenate(held, axis=0)])
    up_grad, down_grad = unpack(where, held, width, ff, plan)
    late, up_grad = behind((late, up_grad))

    late = gather_seg(late)
    big, out, mw_grad, mg_grad, gains_grad, dclass = message_back(
        where, late, forward, message_weight, gain, qkv_weights, out_weights, big, out,
        plan.layout, groups,
    )
    fixed = (dclass + dcls)[:count].astype(bf16).reshape(micro, clips, per_frame, 1, width)
    grad = lax.dynamic_update_slice(grad.reshape(video.shape), fixed, (0, 0, 0, 0, 0))
    return (
        video_out.reshape(video.shape),
        caption_out.reshape(captions.shape),
        grad,
        caption_grad.reshape(captions.shape),
        mw_grad,
        mg_grad,
        big,
        out,
        up_grad,
        down_grad,
        gains_grad,
    )


def solution(mesh):
    rows = P(None, ("clip", "seg"), "frame", None, None)
    caps = P(None, ("clip", "seg"), "frame", None)
    return jax.shard_map(
        local,
        mesh=mesh,
        in_specs=(rows, caps, P(None, ("clip", "seg"), None)) + (P(),) * 7 + (rows, caps),
        out_specs=(rows, caps, rows, caps) + (P(),) * 7,
        check_vma=False,
    )
```

profile of v0, /device:TPU:0, one launch (start us, length us, event | category | flops | bytes accessed | tf_op | source)
XLA Modules:
  0.0 177.2 jit_solution(547330630721308190)
XLA Ops:
  2.0 3.9 %collective-permute-start.2 = (bf16[16,384]{1,0:T(8,128)(2,1)}, bf16[16,384]{1,0:T(8,128)(2,1)}, u32[]{:S(2)}, u32[]{:S(2)}) collective-permute-start(bf16[16,384]{1,0:T(8,128)(2,1)} %class_rows.1.refs_0_), channel_id=1, source_target_pairs={{0,6},{2,4},{4,2},{6,0},{1,7},{3,5},{5,3},{7,1},{8,14},{10,12},{12... | collective-permute-start | bytes 36872 | tf_op jit(solution)/shard_map/ppermute | solution.py:1096
  6.5 1.6 copy.35
  8.1 2.9 %norm_tokens.1 = (bf16[10,208,384]{2,1,0:T(8,128)(2,1)S(1)}, bf16[10,208,768]{2,1,0:T(8,128)(2,1)S(1)}) custom-call(bf16[10,197,384]{2,1,0:T(8,128)(2,1)S(1)} %bitcast.104, f32[4,384]{1,0:T(4,128)S(1)} %copy-done.24, bf16[3,3,384,384]{3,2,1,0:T(8,128)(2,1)S(1)} %copy-done, bf16[3,3,384,384]{3,2,1,0:T(8,128)(2,1)S(1)} %copy-done), custom_call_target="tpu_custom_call" | custom-call | flops 1226833920 | bytes 6389760 | tf_op jit(solution)/shard_map/norm_tokens/pallas_call | solution.py:178
  11.1 1.7 copy-done.31
  15.6 1.9 %copy-done.32 = bf16[10,208,768]{2,1,0:T(8,128)(2,1)S(1)} copy-done((bf16[10,208,768]{2,1,0:T(8,128)(2,1)S(1)}, bf16[10,208,768]{2,1,0:T(8,128)(2,1)}, u32[]{:S(2)}) %copy-start.32) | copy-done | bytes 3194904
  20.1 4.5 %first_rows.1 = (f32[16,384]{1,0:T(8,128)S(1)}, f32[16,384]{1,0:T(8,128)S(1)}, f32[16,768]{1,0:T(8,128)S(1)}, bf16[16,384]{1,0:T(8,128)(2,1)S(1)}, f32[16,384]{1,0:T(8,128)S(1)}) custom-call(bf16[16,384]{1,0:T(8,128)(2,1)S(1)} %copy-done.17, bf16[16,384]{1,0:T(8,128)(2,1)} %collective-permute-done.refs_1_, bf16[16,384]{1,0:T(8,128)(2,1)} %collective-permute-done.1.refs_2_, ...), custom_call_target="tpu_custom_call" | custom-call | flops 4000000000 | bytes 12000000 | tf_op jit(solution)/shard_map/first_rows/pallas_call | solution.py:286
  24.6 2.9 %collective-permute-start.5 = (bf16[16,384]{1,0:T(8,128)(2,1)S(1)}, bf16[16,384]{1,0:T(8,128)(2,1)S(1)}, u32[]{:S(2)}, u32[]{:S(2)}) collective-permute-start(bf16[16,384]{1,0:T(8,128)(2,1)S(1)} %get-tuple-element.152.refs_0_), channel_id=1, source_target_pairs={{0,6},{2,4},{4,2},{6,0},{1,7},{3,5},{5,3},{7,1},{8,14},{10,12},{12... | collective-permute-start | bytes 36872 | tf_op jit(solution)/shard_map/ppermute | solution.py:1096
  29.2 2.0 %collective-permute-done.4.refs_2_ = bf16[16,384]{1,0:T(8,128)(2,1)S(1)} collective-permute-done((bf16[16,384]{1,0:T(8,128)(2,1)S(1)}, bf16[16,384]{1,0:T(8,128)(2,1)S(1)}, u32[]{:S(2)}, u32[]{:S(2)}) %collective-permute-start.4) | collective-permute-done | bytes 12320 | tf_op jit(solution)/shard_map/ppermute | solution.py:1096
  31.7 3.8 %captions_step.1 = (bf16[64,384]{1,0:T(8,128)(2,1)}, bf16[64,384]{1,0:T(8,128)(2,1)}, f32[8,384]{1,0:T(8,128)S(1)}, f32[16,384]{1,0:T(8,128)S(1)}, f32[16,384]{1...) custom-call(s32[3]{0:T(128)S(1)} %pad_add_fusion.where_ref, ...), custom_call_target="tpu_custom_call" | custom-call | flops 4000000000 | bytes 8000000 | tf_op jit(solution)/shard_map/captions_step/pallas_call | solution.py:521
  37.4 1.9 %collective-permute-start.7 = (f32[16,384]{1,0:T(8,128)S(1)}, f32[16,384]{1,0:T(8,128)S(1)}, u32[]{:S(2)}, u32[]{:S(2)}) collective-permute-start(f32[16,384]{1,0:T(8,128)S(1)} %get-tuple-element.155), channel_id=1, source_target_pairs={{0,4},{2,6},{4,0},{6,2},{1,5},{3,7},{5,1},{7,3},{8,12},{10,14},{12... | collective-permute-start | bytes 73736 | tf_op jit(solution)/shard_map/ppermute | solution.py:1096
  40.9 1.6 collective-permute-start.12
  42.6 1.9 %collective-permute-start.10 = (bf16[4,48,384]{2,1,0:T(8,128)(2,1)S(1)}, bf16[4,48,384]{2,1,0:T(8,128)(2,1)S(1)}, u32[]{:S(2)}, u32[]{:S(2)}) collective-permute-start(bf16[4,48,384]{2,1,0:T(8,128)(2,1)S(1)} %get-tuple-element.321.refs_0_), channel_id=1, source_target_pairs={{0,2},{2,0},{4,6},{6,4},{1,3},{3,1},{5,7},{7,5},{8,10},{10,8},{12,... | collective-permute-start | bytes 442376 | tf_op jit(solution)/shard_map/ppermute | solution.py:1096
  44.5 9.1 %attend.1 = (f32[10,208,384]{2,1,0:T(8,128)S(1)}, bf16[10,384,208]{2,1,0:T(8,128)(2,1)S(1)}, f32[10,8,208]{2,1,0:T(8,128)S(1)}) custom-call(bf16[10,208,384]{2,1,0:T(8,128)(2,1)S(1)} %copy-done.35, bf16[10,208,768]{2,1,0:T(8,128)(2,1)S(1)} %copy-done.33, bf16[10,197,384]{2,1,0:T(8,128)(2,1)S(1)} %bitcast.105, ...), custom_call_target="tpu_custom_call" | custom-call | flops 14000000000 | bytes 10000000 | tf_op jit(solution)/shard_map/attend/pallas_call | solution.py:401
  53.8 1.6 collective-permute-start.13
  55.5 24.5 %mlp_step.1 = (bf16[10,197,384]{2,1,0:T(8,128)(2,1)S(1)}, f32[10,208,384]{2,1,0:T(8,128)S(1)}, f32[8,384]{1,0:T(8,128)S(1)}, bf16[4,4,48,768]{3,2,1,0:T(8,128)(2,1)S(1)}, bf16[4,4,48,768]{3,2,1,0:T(8,128)(2,1)S(1)}) custom-call(s32[3]{0:T(128)S(1)} %pad_add_fusion.where_ref, f32[10,208,384]{2,1,0:T(8,128)S(1)} %get-tuple-element.173.resid_ref, ...), custom_call_target="tpu_custom_call" | custom-call | flops 20000000000 | bytes 20000000 | tf_op jit(solution)/shard_map/mlp_step/pallas_call | solution.py:612
  80.2 2.3 %copy.44 = bf16[2,5,1,197,384]{4,0,3,2,1:T(2,128)(2,1)} copy(bf16[2,5,1,197,384]{4,3,1,0,2:T(8,128)(2,1)S(1)} %bitcast.111) | data formatting | bytes 3025920 | tf_op jit(solution)/shard_map/reshape | solution.py:1319
  83.3 2.6 %collective-permute-start.18 = (bf16[320,384]{1,0:T(8,128)(2,1)S(1)}, bf16[320,384]{1,0:T(8,128)(2,1)S(1)}, u32[]{:S(2)}, u32[]{:S(2)}) collective-permute-start(bf16[320,384]{1,0:T(8,128)(2,1)S(1)} %pad_maximum_fusion.2), channel_id=1, source_target_pairs={{0,16},{8,24},{16,0},{24,8},{1,17},{9,25},{17,1},{25,9},{2,18},{10... | collective-permute-start | bytes 737288 | tf_op jit(solution)/shard_map/ppermute | solution.py:1096
  89.5 13.1 %attend_back.2 = (bf16[10,197,384]{2,1,0:T(8,128)(2,1)S(1)}, f32[16,384]{1,0:T(8,128)S(1)}, f32[16,384]{1,0:T(8,128)S(1)}, f32[8,384]{1,0:T(8,128)S(1)}, f32[1536,384]{1,0:T(8,128)S(1)}) custom-call(s32[3]{0:T(128)S(1)} %pad_add_fusion.where_ref, bf16[10,208,384]{2,1,0:T(8,128)(2,1)S(1)} %copy-done.35, bf16[10,208,768]{2,1,0:T(8,128)(2,1)S(1)} %copy-done.33, ...), custom_call_target="tpu_custom_call" | custom-call | flops 13500000256 | bytes 12000000 | tf_op jit(solution)/shard_map/attend_back/pallas_call | solution.py:752
  102.9 1.5 collective-permute-start.22
  106.9 9.8 %attend_back.3 = (bf16[10,197,384]{2,1,0:T(8,128)(2,1)S(1)}, f32[16,384]{1,0:T(8,128)S(1)}, f32[16,384]{1,0:T(8,128)S(1)}, f32[8,384]{1,0:T(8,128)S(1)}, bf16[4,...) custom-call(s32[3]{0:T(128)S(1)} %pad_add_fusion.where_ref, ...), custom_call_target="tpu_custom_call", output_to_operand_aliasing={{0}: (15, {})} | custom-call | flops 8999999488 | bytes 8000000 | tf_op jit(solution)/shard_map/attend_back/pallas_call | solution.py:752
  121.7 1.6 collective-permute-start.27
  123.5 1.8 collective-permute-start.25
  125.3 9.8 %collective-permute-done.23 = bf16[4,48,768]{2,1,0:T(8,128)(2,1)S(1)} collective-permute-done((bf16[4,48,768]{2,1,0:T(8,128)(2,1)S(1)}, bf16[4,48,768]{2,1,0:T(8,128)(2,1)S(1)}, u32[]{:S(2)}, u32[]{:S(2)}) %collective-permute-start.23) | collective-permute-done | bytes 294944 | tf_op jit(solution)/shard_map/ppermute | solution.py:1096
  137.2 1.5 collective-permute-start.31
  140.7 2.0 %collective-permute-done.32 = bf16[208,384]{1,0:T(8,128)(2,1)S(1)} collective-permute-done((bf16[208,384]{1,0:T(8,128)(2,1)S(1)}, bf16[208,384]{1,0:T(8,128)(2,1)S(1)}, u32[]{:S(2)}, u32[]{:S(2)}) %collective-permute-start.32) | collective-permute-done | bytes 159776 | tf_op jit(solution)/shard_map/ppermute | solution.py:1096
  143.5 5.4 %message_forward.1 = (bf16[1,512,384]{2,1,0:T(8,128)(2,1)}, bf16[1,512,384]{2,1,0:T(8,128)(2,1)}, bf16[1,512,384]{2,1,0:T(8,128)(2,1)}, bf16[1,384,512]{2,1,0:T(...) custom-call(s32[3]{0:T(128)} %copy-done.29, ...), custom_call_target="tpu_custom_call" | custom-call | flops 3000000000 | bytes 6000000 | tf_op jit(solution)/shard_map/message_forward/pallas_call | solution.py:911
  148.9 2.2 %unpack_side.1 = (f32[3,3,384,384]{3,2,1,0:T(8,128)}, f32[3,384,384]{2,1,0:T(8,128)}) custom-call(s32[3]{0:T(128)S(1)} %copy-done.30, bf16[4,4,48,384]{3,2,1,0:T(8,128)(2,1)S(1)} %pad_maximum_fusion.1.refs_0_, bf16[4,4,48,384]{3,2,1,0:T(8,128)(2,1)S(1)} %bitcast.112), custom_call_target="tpu_custom_call" | custom-call | flops 1000000000 | bytes 4000000 | tf_op jit(solution)/shard_map/unpack_side/pallas_call | solution.py:1226
  156.8 3.3 %unpack.1 = (f32[384,1536]{1,0:T(8,128)}, f32[1536,384]{1,0:T(8,128)}) custom-call(s32[3]{0:T(128)S(1)} %copy-done.30, bf16[16,48,768]{2,1,0:T(8,128)(2,1)S(1)} %constant_dynamic-update-slice_fusion.refs_0_, bf16[16,48,768]{2,1,0:T(8,128)(2,1)S(1)} %collective-permute-done.37.refs_1_), custom_call_target="tpu_custom_call" | custom-call | flops 2000000000 | bytes 10000000 | tf_op jit(solution)/shard_map/unpack/pallas_call | solution.py:1200
  160.1 1.8 %collective-permute-done.36.refs_3_ = bf16[256,384]{1,0:T(8,128)(2,1)S(1)} collective-permute-done((bf16[256,384]{1,0:T(8,128)(2,1)S(1)}, bf16[256,384]{1,0:T(8,128)(2,1)S(1)}, u32[]{:S(2)}, u32[]{:S(2)}) %collective-permute-start.36) | collective-permute-done | bytes 196640 | tf_op jit(solution)/shard_map/ppermute | solution.py:1096
  161.9 3.8 %collective-permute-done.35.refs_2_ = bf16[256,384]{1,0:T(8,128)(2,1)S(1)} collective-permute-done((bf16[256,384]{1,0:T(8,128)(2,1)S(1)}, bf16[256,384]{1,0:T(8,128)(2,1)S(1)}, u32[]{:S(2)}, u32[]{:S(2)}) %collective-permute-start.35) | collective-permute-done | bytes 196640 | tf_op jit(solution)/shard_map/ppermute | solution.py:1096
  166.7 2.3 %copy.38 = bf16[2,5,1,197,384]{4,0,3,2,1:T(2,128)(2,1)} copy(bf16[2,5,1,197,384]{4,3,1,0,2:T(8,128)(2,1)S(1)} %bitcast.110) | data formatting | bytes 3025920 | tf_op jit(solution)/shard_map/reshape | solution.py:1374
  169.2 7.4 %message_back.1 = (f32[3,3,384,384]{3,2,1,0:T(8,128)}, f32[3,384,384]{2,1,0:T(8,128)}, f32[384,384]{1,0:T(8,128)}, f32[384]{0:T(512)}, f32[4,384]{1,0:T(4,128)}, /*index=5*/f32[16,384]{1,0:T(8,128)S(1)}) custom-call(s32[3]{0:T(128)S(1)} %copy-done.30, ...), custom_call_target="tpu_custom_call", output_to_operand_aliasing={{0}: (20, {}), {1}: (21, {})} | custom-call | flops 4000000000 | bytes 12000000 | tf_op jit(solution)/shard_map/message_back/pallas_call | solution.py:1024
  (206 shorter events, 37.7 us)
Async XLA Ops:
  2.0 11.9 %collective-permute-start.2 = (bf16[16,384]{1,0:T(8,128)(2,1)}, bf16[16,384]{1,0:T(8,128)(2,1)}, u32[]{:S(2)}, u32[]{:S(2)}) collective-permute-start(bf16[16,384]{1,0:T(8,128)(2,1)} %class_rows.1.refs_0_), channel_id=1, source_target_pairs={{0,6},{2,4},{4,2},{6,0},{1,7},{3,5},{5,3},{7,1},{8,14},{10,12},{12... | collective-permute-start | bytes 36872 | tf_op jit(solution)/shard_map/ppermute | solution.py:1096
  5.8 8.1 %collective-permute-start.1 = (bf16[16,384]{1,0:T(8,128)(2,1)}, bf16[16,384]{1,0:T(8,128)(2,1)}, u32[]{:S(2)}, u32[]{:S(2)}) collective-permute-start(bf16[16,384]{1,0:T(8,128)(2,1)} %class_rows.1.refs_0_), channel_id=1, source_target_pairs={{0,4},{2,6},{4,0},{6,2},{1,5},{3,7},{5,1},{7,3},{8,12},{10,14},{12... | collective-permute-start | bytes 36872 | tf_op jit(solution)/shard_map/ppermute | solution.py:1096
  6.4 7.6 %collective-permute-start = (bf16[16,384]{1,0:T(8,128)(2,1)}, bf16[16,384]{1,0:T(8,128)(2,1)}, u32[]{:S(2)}, u32[]{:S(2)}) collective-permute-start(bf16[16,384]{1,0:T(8,128)(2,1)} %class_rows.1.refs_0_), channel_id=1, source_target_pairs={{0,2},{2,0},{4,6},{6,4},{1,3},{3,1},{5,7},{7,5},{8,10},{10,8},{12,... | collective-permute-start | bytes 36872 | tf_op jit(solution)/shard_map/ppermute | solution.py:1096
  36.1 4.7 %collective-permute-start.9 = (bf16[4,4,48,384]{3,2,1,0:T(8,128)(2,1)S(1)}, bf16[4,4,48,384]{3,2,1,0:T(8,128)(2,1)S(1)}, u32[]{:S(2)}, u32[]{:S(2)}) collective-permute-start(bf16[4,4,48,384]{3,2,1,0:T(8,128)(2,1)S(1)} %get-tuple-element.162), channel_id=1, source_target_pairs={{0,1},{1,0},{2,3},{3,2},{4,5},{5,4},{6,7},{7,6},{8,9},{9,8},{10,11... | collective-permute-start | bytes 1769480 | tf_op jit(solution)/shard_map/ppermute | solution.py:1096
  37.2 5.3 %collective-permute-start.6 = (f32[16,384]{1,0:T(8,128)S(1)}, f32[16,384]{1,0:T(8,128)S(1)}, u32[]{:S(2)}, u32[]{:S(2)}) collective-permute-start(f32[16,384]{1,0:T(8,128)S(1)} %get-tuple-element.154), channel_id=1, source_target_pairs={{0,2},{2,0},{4,6},{6,4},{1,3},{3,1},{5,7},{7,5},{8,10},{10,8},{12,... | collective-permute-start | bytes 73736 | tf_op jit(solution)/shard_map/ppermute | solution.py:1096
  37.4 16.2 %collective-permute-start.7 = (f32[16,384]{1,0:T(8,128)S(1)}, f32[16,384]{1,0:T(8,128)S(1)}, u32[]{:S(2)}, u32[]{:S(2)}) collective-permute-start(f32[16,384]{1,0:T(8,128)S(1)} %get-tuple-element.155), channel_id=1, source_target_pairs={{0,4},{2,6},{4,0},{6,2},{1,5},{3,7},{5,1},{7,3},{8,12},{10,14},{12... | collective-permute-start | bytes 73736 | tf_op jit(solution)/shard_map/ppermute | solution.py:1096
  39.3 14.3 %collective-permute-start.8 = (f32[16,384]{1,0:T(8,128)S(1)}, f32[16,384]{1,0:T(8,128)S(1)}, u32[]{:S(2)}, u32[]{:S(2)}) collective-permute-start(f32[16,384]{1,0:T(8,128)S(1)} %get-tuple-element.156), channel_id=1, source_target_pairs={{0,6},{2,4},{4,2},{6,0},{1,7},{3,5},{5,3},{7,1},{8,14},{10,12},{12... | collective-permute-start | bytes 73736 | tf_op jit(solution)/shard_map/ppermute | solution.py:1096
  40.9 12.7 %collective-permute-start.12 = (bf16[4,48,384]{2,1,0:T(8,128)(2,1)S(1)}, bf16[4,48,384]{2,1,0:T(8,128)(2,1)S(1)}, u32[]{:S(2)}, u32[]{:S(2)}) collective-permute-start(bf16[4,48,384]{2,1,0:T(8,128)(2,1)S(1)} %get-tuple-element.319.refs_2_), channel_id=1, source_target_pairs={{0,6},{2,4},{4,2},{6,0},{1,7},{3,5},{5,3},{7,1},{8,14},{10,12},{12... | collective-permute-start | bytes 442376 | tf_op jit(solution)/shard_map/ppermute | solution.py:1096
  42.5 11.2 %collective-permute-start.11 = (bf16[4,48,384]{2,1,0:T(8,128)(2,1)S(1)}, bf16[4,48,384]{2,1,0:T(8,128)(2,1)S(1)}, u32[]{:S(2)}, u32[]{:S(2)}) collective-permute-start(bf16[4,48,384]{2,1,0:T(8,128)(2,1)S(1)} %get-tuple-element.320.refs_1_), channel_id=1, source_target_pairs={{0,4},{2,6},{4,0},{6,2},{1,5},{3,7},{5,1},{7,3},{8,12},{10,14},{12... | collective-permute-start | bytes 442376 | tf_op jit(solution)/shard_map/ppermute | solution.py:1096
  42.6 11.1 %collective-permute-start.10 = (bf16[4,48,384]{2,1,0:T(8,128)(2,1)S(1)}, bf16[4,48,384]{2,1,0:T(8,128)(2,1)S(1)}, u32[]{:S(2)}, u32[]{:S(2)}) collective-permute-start(bf16[4,48,384]{2,1,0:T(8,128)(2,1)S(1)} %get-tuple-element.321.refs_0_), channel_id=1, source_target_pairs={{0,2},{2,0},{4,6},{6,4},{1,3},{3,1},{5,7},{7,5},{8,10},{10,8},{12,... | collective-permute-start | bytes 442376 | tf_op jit(solution)/shard_map/ppermute | solution.py:1096
  53.8 26.2 %collective-permute-start.13 = (bf16[256,384]{1,0:T(8,128)(2,1)S(1)}, bf16[256,384]{1,0:T(8,128)(2,1)S(1)}, u32[]{:S(2)}, u32[]{:S(2)}) collective-permute-start(bf16[256,384]{1,0:T(8,128)(2,1)S(1)} %pad_maximum_fusion.3), channel_id=1, source_target_pairs={{0,8},{8,0},{16,24},{24,16},{1,9},{9,1},{17,25},{25,17},{2,10},{10... | collective-permute-start | bytes 589832 | tf_op jit(solution)/shard_map/ppermute | solution.py:1096
  83.3 19.2 %collective-permute-start.18 = (bf16[320,384]{1,0:T(8,128)(2,1)S(1)}, bf16[320,384]{1,0:T(8,128)(2,1)S(1)}, u32[]{:S(2)}, u32[]{:S(2)}) collective-permute-start(bf16[320,384]{1,0:T(8,128)(2,1)S(1)} %pad_maximum_fusion.2), channel_id=1, source_target_pairs={{0,16},{8,24},{16,0},{24,8},{1,17},{9,25},{17,1},{25,9},{2,18},{10... | collective-permute-start | bytes 737288 | tf_op jit(solution)/shard_map/ppermute | solution.py:1096
  86.0 16.7 %collective-permute-start.15 = (bf16[4,48,768]{2,1,0:T(8,128)(2,1)S(1)}, bf16[4,48,768]{2,1,0:T(8,128)(2,1)S(1)}, u32[]{:S(2)}, u32[]{:S(2)}) collective-permute-start(bf16[4,48,768]{2,1,0:T(8,128)(2,1)S(1)} %get-tuple-element.202), channel_id=1, source_target_pairs={{0,2},{2,0},{4,6},{6,4},{1,3},{3,1},{5,7},{7,5},{8,10},{10,8},{12,... | collective-permute-start | bytes 884744 | tf_op jit(solution)/shard_map/ppermute | solution.py:1096
  86.5 16.2 %collective-permute-start.16 = (bf16[4,48,768]{2,1,0:T(8,128)(2,1)S(1)}, bf16[4,48,768]{2,1,0:T(8,128)(2,1)S(1)}, u32[]{:S(2)}, u32[]{:S(2)}) collective-permute-start(bf16[4,48,768]{2,1,0:T(8,128)(2,1)S(1)} %get-tuple-element.203), channel_id=1, source_target_pairs={{0,4},{2,6},{4,0},{6,2},{1,5},{3,7},{5,1},{7,3},{8,12},{10,14},{12... | collective-permute-start | bytes 884744 | tf_op jit(solution)/shard_map/ppermute | solution.py:1096
  88.0 14.7 %collective-permute-start.17 = (bf16[4,48,768]{2,1,0:T(8,128)(2,1)S(1)}, bf16[4,48,768]{2,1,0:T(8,128)(2,1)S(1)}, u32[]{:S(2)}, u32[]{:S(2)}) collective-permute-start(bf16[4,48,768]{2,1,0:T(8,128)(2,1)S(1)} %get-tuple-element.204), channel_id=1, source_target_pairs={{0,6},{2,4},{4,2},{6,0},{1,7},{3,5},{5,3},{7,1},{8,14},{10,12},{12... | collective-permute-start | bytes 884744 | tf_op jit(solution)/shard_map/ppermute | solution.py:1096
  102.9 14.0 %collective-permute-start.22 = (bf16[4,48,384]{2,1,0:T(8,128)(2,1)S(1)}, bf16[4,48,384]{2,1,0:T(8,128)(2,1)S(1)}, u32[]{:S(2)}, u32[]{:S(2)}) collective-permute-start(bf16[4,48,384]{2,1,0:T(8,128)(2,1)S(1)} %fusion.8), channel_id=1, source_target_pairs={{0,6},{2,4},{4,2},{6,0},{1,7},{3,5},{5,3},{7,1},{8,14},{10,12},{12... | collective-permute-start | bytes 442376 | tf_op jit(solution)/shard_map/ppermute | solution.py:1096
  104.5 12.4 %collective-permute-start.21 = (bf16[4,48,384]{2,1,0:T(8,128)(2,1)S(1)}, bf16[4,48,384]{2,1,0:T(8,128)(2,1)S(1)}, u32[]{:S(2)}, u32[]{:S(2)}) collective-permute-start(bf16[4,48,384]{2,1,0:T(8,128)(2,1)S(1)} %fusion.8), channel_id=1, source_target_pairs={{0,4},{2,6},{4,0},{6,2},{1,5},{3,7},{5,1},{7,3},{8,12},{10,14},{12... | collective-permute-start | bytes 442376 | tf_op jit(solution)/shard_map/ppermute | solution.py:1096
  105.0 12.0 %collective-permute-start.20 = (bf16[4,48,384]{2,1,0:T(8,128)(2,1)S(1)}, bf16[4,48,384]{2,1,0:T(8,128)(2,1)S(1)}, u32[]{:S(2)}, u32[]{:S(2)}) collective-permute-start(bf16[4,48,384]{2,1,0:T(8,128)(2,1)S(1)} %fusion.8), channel_id=1, source_target_pairs={{0,2},{2,0},{4,6},{6,4},{1,3},{3,1},{5,7},{7,5},{8,10},{10,8},{12,... | collective-permute-start | bytes 442376 | tf_op jit(solution)/shard_map/ppermute | solution.py:1096
  106.5 10.3 %collective-permute-start.19 = (bf16[4,48,768]{2,1,0:T(8,128)(2,1)S(1)}, bf16[4,48,768]{2,1,0:T(8,128)(2,1)S(1)}, u32[]{:S(2)}, u32[]{:S(2)}) collective-permute-start(bf16[4,48,768]{2,1,0:T(8,128)(2,1)S(1)} %fusion.2), channel_id=1, source_target_pairs={{0,8},{8,0},{16,24},{24,16},{1,9},{9,1},{17,25},{25,17},{2,10},{10... | collective-permute-start | bytes 884744 | tf_op jit(solution)/shard_map/ppermute | solution.py:1096
  118.4 16.8 %collective-permute-start.28 = (bf16[1024,384]{1,0:T(8,128)(2,1)}, bf16[1024,384]{1,0:T(8,128)(2,1)S(1)}, u32[]{:S(2)}, u32[]{:S(2)}) collective-permute-start(bf16[1024,384]{1,0:T(8,128)(2,1)} %pad_maximum_fusion), channel_id=1, source_target_pairs={{0,1},{1,0},{2,3},{3,2},{4,5},{5,4},{6,7},{7,6},{8,9},{9,8},{10,11... | collective-permute-start | bytes 2359304 | tf_op jit(solution)/shard_map/ppermute | solution.py:1096
  118.7 16.5 %collective-permute-start.23 = (bf16[4,48,768]{2,1,0:T(8,128)(2,1)S(1)}, bf16[4,48,768]{2,1,0:T(8,128)(2,1)S(1)}, u32[]{:S(2)}, u32[]{:S(2)}) collective-permute-start(bf16[4,48,768]{2,1,0:T(8,128)(2,1)S(1)} %add_convert_fusion.1), channel_id=1, source_target_pairs={{0,16},{8,24},{16,0},{24,8},{1,17},{9,25},{17,1},{25,9},{2,18},{10... | collective-permute-start | bytes 884744 | tf_op jit(solution)/shard_map/ppermute | solution.py:1096
  121.7 14.2 %collective-permute-start.27 = (bf16[4,48,384]{2,1,0:T(8,128)(2,1)S(1)}, bf16[4,48,384]{2,1,0:T(8,128)(2,1)S(1)}, u32[]{:S(2)}, u32[]{:S(2)}) collective-permute-start(bf16[4,48,384]{2,1,0:T(8,128)(2,1)S(1)} %get-tuple-element.316), channel_id=1, source_target_pairs={{0,6},{2,4},{4,2},{6,0},{1,7},{3,5},{5,3},{7,1},{8,14},{10,12},{12... | collective-permute-start | bytes 442376 | tf_op jit(solution)/shard_map/ppermute | solution.py:1096
  123.3 12.7 %collective-permute-start.26 = (bf16[4,48,384]{2,1,0:T(8,128)(2,1)S(1)}, bf16[4,48,384]{2,1,0:T(8,128)(2,1)S(1)}, u32[]{:S(2)}, u32[]{:S(2)}) collective-permute-start(bf16[4,48,384]{2,1,0:T(8,128)(2,1)S(1)} %get-tuple-element.317), channel_id=1, source_target_pairs={{0,4},{2,6},{4,0},{6,2},{1,5},{3,7},{5,1},{7,3},{8,12},{10,14},{12... | collective-permute-start | bytes 442376 | tf_op jit(solution)/shard_map/ppermute | solution.py:1096
  123.5 12.4 %collective-permute-start.25 = (bf16[4,48,384]{2,1,0:T(8,128)(2,1)S(1)}, bf16[4,48,384]{2,1,0:T(8,128)(2,1)S(1)}, u32[]{:S(2)}, u32[]{:S(2)}) collective-permute-start(bf16[4,48,384]{2,1,0:T(8,128)(2,1)S(1)} %get-tuple-element.318), channel_id=1, source_target_pairs={{0,2},{2,0},{4,6},{6,4},{1,3},{3,1},{5,7},{7,5},{8,10},{10,8},{12,... | collective-permute-start | bytes 442376 | tf_op jit(solution)/shard_map/ppermute | solution.py:1096
  137.1 5.6 %collective-permute-start.32 = (bf16[208,384]{1,0:T(8,128)(2,1)S(1)}, bf16[208,384]{1,0:T(8,128)(2,1)S(1)}, u32[]{:S(2)}, u32[]{:S(2)}) collective-permute-start(bf16[208,384]{1,0:T(8,128)(2,1)S(1)} %pad_maximum_fusion.7), channel_id=1, source_target_pairs={{0,8},{8,0},{16,24},{24,16},{1,9},{9,1},{17,25},{25,17},{2,10},{10... | collective-permute-start | bytes 479240 | tf_op jit(solution)/shard_map/ppermute | solution.py:1096
  137.2 15.3 %collective-permute-start.31 = (bf16[4,48,768]{2,1,0:T(8,128)(2,1)S(1)}, bf16[4,48,768]{2,1,0:T(8,128)(2,1)S(1)}, u32[]{:S(2)}, u32[]{:S(2)}) collective-permute-start(bf16[4,48,768]{2,1,0:T(8,128)(2,1)S(1)} %add_convert_fusion), channel_id=1, source_target_pairs={{0,6},{2,4},{4,2},{6,0},{1,7},{3,5},{5,3},{7,1},{8,14},{10,12},{12... | collective-permute-start | bytes 884744 | tf_op jit(solution)/shard_map/ppermute | solution.py:1096
  138.7 14.2 %collective-permute-start.30 = (bf16[4,48,768]{2,1,0:T(8,128)(2,1)S(1)}, bf16[4,48,768]{2,1,0:T(8,128)(2,1)S(1)}, u32[]{:S(2)}, u32[]{:S(2)}) collective-permute-start(bf16[4,48,768]{2,1,0:T(8,128)(2,1)S(1)} %add_convert_fusion), channel_id=1, source_target_pairs={{0,4},{2,6},{4,0},{6,2},{1,5},{3,7},{5,1},{7,3},{8,12},{10,14},{12... | collective-permute-start | bytes 884744 | tf_op jit(solution)/shard_map/ppermute | solution.py:1096
  139.2 13.8 %collective-permute-start.29 = (bf16[4,48,768]{2,1,0:T(8,128)(2,1)S(1)}, bf16[4,48,768]{2,1,0:T(8,128)(2,1)S(1)}, u32[]{:S(2)}, u32[]{:S(2)}) collective-permute-start(bf16[4,48,768]{2,1,0:T(8,128)(2,1)S(1)} %add_convert_fusion), channel_id=1, source_target_pairs={{0,2},{2,0},{4,6},{6,4},{1,3},{3,1},{5,7},{7,5},{8,10},{10,8},{12,... | collective-permute-start | bytes 884744 | tf_op jit(solution)/shard_map/ppermute | solution.py:1096
  142.8 9.5 %collective-permute-start.33 = (bf16[224,384]{1,0:T(8,128)(2,1)S(1)}, bf16[224,384]{1,0:T(8,128)(2,1)S(1)}, u32[]{:S(2)}, u32[]{:S(2)}) collective-permute-start(bf16[224,384]{1,0:T(8,128)(2,1)S(1)} %pad_maximum_fusion.6), channel_id=1, source_target_pairs={{0,16},{8,24},{16,0},{24,8},{1,17},{9,25},{17,1},{25,9},{2,18},{10... | collective-permute-start | bytes 516104 | tf_op jit(solution)/shard_map/ppermute | solution.py:1096
  153.2 8.7 %collective-permute-start.36 = (bf16[256,384]{1,0:T(8,128)(2,1)S(1)}, bf16[256,384]{1,0:T(8,128)(2,1)S(1)}, u32[]{:S(2)}, u32[]{:S(2)}) collective-permute-start(bf16[256,384]{1,0:T(8,128)(2,1)S(1)} %pad_maximum_fusion.5.refs_0_), channel_id=1, source_target_pairs={{0,6},{2,4},{4,2},{6,0},{1,7},{3,5},{5,3},{7,1},{8,14},{10,12},{12... | collective-permute-start | bytes 589832 | tf_op jit(solution)/shard_map/ppermute | solution.py:1096
  154.7 11.0 %collective-permute-start.35 = (bf16[256,384]{1,0:T(8,128)(2,1)S(1)}, bf16[256,384]{1,0:T(8,128)(2,1)S(1)}, u32[]{:S(2)}, u32[]{:S(2)}) collective-permute-start(bf16[256,384]{1,0:T(8,128)(2,1)S(1)} %pad_maximum_fusion.5.refs_0_), channel_id=1, source_target_pairs={{0,4},{2,6},{4,0},{6,2},{1,5},{3,7},{5,1},{7,3},{8,12},{10,14},{12... | collective-permute-start | bytes 589832 | tf_op jit(solution)/shard_map/ppermute | solution.py:1096
  155.3 10.4 %collective-permute-start.34 = (bf16[256,384]{1,0:T(8,128)(2,1)S(1)}, bf16[256,384]{1,0:T(8,128)(2,1)S(1)}, u32[]{:S(2)}, u32[]{:S(2)}) collective-permute-start(bf16[256,384]{1,0:T(8,128)(2,1)S(1)} %pad_maximum_fusion.5.refs_0_), channel_id=1, source_target_pairs={{0,2},{2,0},{4,6},{6,4},{1,3},{3,1},{5,7},{7,5},{8,10},{10,8},{12,... | collective-permute-start | bytes 589832 | tf_op jit(solution)/shard_map/ppermute | solution.py:1096
  (57 other events, 426.5 us)
where the time goes:
time: 178 us; the launch traced here: 177 us
  Pallas kernels  88.8 us (50%)
  starting transfers between devices  40.2 us (23%)
  waiting for transfers between devices  23.2 us (13%)
  local copies, waits for them, and re-layouts  17.6 us (10%)
  other arithmetic  5.9 us (3%)
    ppermute x42, starting transfers between devices, swap(): return lax.ppermute(x, axis, [(i, i ^ k) for i in range(count)])  40.2 us
    pallas_call x1, Pallas kernels, mlp_step(): pl.pallas_call(functools.partial(mlp_kernel, len(parts), patch, ff), grid...  24.5 us
    ppermute x42, waiting for transfers between devices, swap(): return lax.ppermute(x, axis, [(i, i ^ k) for i in range(count)])  23.2 us
    pallas_call x2, Pallas kernels, attend_back(): pl.pallas_call(functools.partial(attend_back_kernel, patch + 1, first, la...  22.9 us
    unnamed x99, local copies, waits for them, and re-layouts  11.5 us
    pallas_call x1, Pallas kernels, attend(): pl.pallas_call(functools.partial(attend_kernel, tokens), grid=(count // b...  9.11 us
    pallas_call x1, Pallas kernels, message_back(): pl.pallas_call(functools.partial(message_back_kernel, layout, groups), gr...  7.44 us
    pallas_call x1, Pallas kernels, message_forward(): pl.pallas_call(functools.partial(message_forward_kernel, groups), grid=(1...  5.43 us
  transfers between devices with their start and end apart: 42, of which 11 were waited for; matrix products, arithmetic and copies ran while one was open for 6% of the time, Pallas kernels for 40%

commit v1 on v0

--- a/solution.py
+++ b/solution.py
@@ -306,7 +306,7 @@
             shape_of((slots, width), f32),
         ],
         scratch_shapes=[pltpu.VMEM((slots, width), f32)],
-        compiler_params=params(16),
+        compiler_params=params(56),
         cost_estimate=cost(4e9, 12e6),
         name="first_rows",
     )(*operands)

time: 178 us -> 176 us (0.989)
  local copies, waits for them, and re-layouts: 17.6 us -> 13.2 us
  Pallas kernels: 88.8 us -> 92 us
    pallas_call x1, Pallas kernels: 4.49 us -> 7.99 us  [first_rows(): pl.pallas_call(functools.partial(first_kernel, len(gathered), count, toke...]
    unnamed x99 -> x115, local copies, waits for them, and re-layouts: 11.5 us -> 8.27 us
  transfers between devices with their start and end apart: 42 -> 42, of which waited for: 11 -> 11; matrix products, arithmetic and copies ran while one was open for 6% -> 5% of each run, Pallas kernels for 40% -> 41%
where the time goes in v1:
time: 176 us
  Pallas kernels  92 us (52%)
  starting transfers between devices  39.9 us (23%)
  waiting for transfers between devices  24 us (14%)
  local copies, waits for them, and re-layouts  13.2 us (8%)
  other arithmetic  4.78 us (3%)
    ppermute x42, starting transfers between devices, swap(): return lax.ppermute(x, axis, [(i, i ^ k) for i in range(count)])  39.9 us
    pallas_call x1, Pallas kernels, mlp_step(): pl.pallas_call(functools.partial(mlp_kernel, len(parts), patch, ff), grid...  24.3 us
    ppermute x42, waiting for transfers between devices, swap(): return lax.ppermute(x, axis, [(i, i ^ k) for i in range(count)])  24 us
    pallas_call x2, Pallas kernels, attend_back(): pl.pallas_call(functools.partial(attend_back_kernel, patch + 1, first, la...  22.9 us
    pallas_call x1, Pallas kernels, attend(): pl.pallas_call(functools.partial(attend_kernel, tokens), grid=(count // b...  9.09 us
    unnamed x115, local copies, waits for them, and re-layouts  8.27 us
    pallas_call x1, Pallas kernels, first_rows(): pl.pallas_call(functools.partial(first_kernel, len(gathered), count, toke...  7.99 us
    pallas_call x1, Pallas kernels, message_back(): pl.pallas_call(functools.partial(message_back_kernel, layout, groups), gr...  7.41 us
  transfers between devices with their start and end apart: 42, of which 11 were waited for; matrix products, arithmetic and copies ran while one was open for 5% of the time, Pallas kernels for 41%

profile of v1, /device:TPU:0, one launch (start us, length us, event | category | flops | bytes accessed | tf_op | source)
XLA Modules:
  0.0 175.5 jit_solution(14420551039630927209)
XLA Ops:
  2.1 3.9 %collective-permute-start.2 = (bf16[16,384]{1,0:T(8,128)(2,1)}, bf16[16,384]{1,0:T(8,128)(2,1)S(1)}, u32[]{:S(2)}, u32[]{:S(2)}) collective-permute-start(bf16[16,384]{1,0:T(8,128)(2,1)} %class_rows.1.refs_0_), channel_id=1, source_target_pairs={{0,6},{2,4},{4,2},{6,0},{1,7},{3,5},{5,3},{7,1},{8,14},{10,12},{12... | collective-permute-start | bytes 36872 | tf_op jit(solution)/shard_map/ppermute | solution.py:1096
  6.8 2.9 %norm_tokens.1 = (bf16[10,208,384]{2,1,0:T(8,128)(2,1)S(1)}, bf16[10,208,768]{2,1,0:T(8,128)(2,1)S(1)}) custom-call(bf16[10,197,384]{2,1,0:T(8,128)(2,1)S(1)} %bitcast.104, f32[4,384]{1,0:T(4,128)S(1)} %copy-done.23, bf16[3,3,384,384]{3,2,1,0:T(8,128)(2,1)S(1)} %copy-done, bf16[3,3,384,384]{3,2,1,0:T(8,128)(2,1)S(1)} %copy-done), custom_call_target="tpu_custom_call" | custom-call | flops 1226833920 | bytes 6389760 | tf_op jit(solution)/shard_map/norm_tokens/pallas_call | solution.py:178
  9.8 1.7 copy-done.28
  13.8 8.0 %first_rows.1 = (f32[16,384]{1,0:T(8,128)}, f32[16,384]{1,0:T(8,128)}, f32[16,768]{1,0:T(8,128)}, bf16[16,384]{1,0:T(8,128)(2,1)}, f32[16,384]{1,0:T(8,128)}) custom-call(bf16[16,384]{1,0:T(8,128)(2,1)} %class_rows.1.refs_0_, bf16[16,384]{1,0:T(8,128)(2,1)} %copy-done.52, bf16[16,384]{1,0:T(8,128)(2,1)} %copy-done.50, bf16[16,384]{1,0:T(8,128)(2,1)} %copy-done.48, ...), custom_call_target="tpu_custom_call" | custom-call | flops 4000000000 | bytes 12000000 | tf_op jit(solution)/shard_map/first_rows/pallas_call | solution.py:286
  21.8 2.9 %collective-permute-start.5 = (bf16[16,384]{1,0:T(8,128)(2,1)}, bf16[16,384]{1,0:T(8,128)(2,1)S(1)}, u32[]{:S(2)}, u32[]{:S(2)}) collective-permute-start(bf16[16,384]{1,0:T(8,128)(2,1)} %get-tuple-element.152.refs_0_), channel_id=1, source_target_pairs={{0,6},{2,4},{4,2},{6,0},{1,7},{3,5},{5,3},{7,1},{8,14},{10,12},{12... | collective-permute-start | bytes 36872 | tf_op jit(solution)/shard_map/ppermute | solution.py:1096
  26.6 2.0 %collective-permute-done.4.refs_2_ = bf16[16,384]{1,0:T(8,128)(2,1)S(1)} collective-permute-done((bf16[16,384]{1,0:T(8,128)(2,1)}, bf16[16,384]{1,0:T(8,128)(2,1)S(1)}, u32[]{:S(2)}, u32[]{:S(2)}) %collective-permute-start.4) | collective-permute-done | bytes 12320 | tf_op jit(solution)/shard_map/ppermute | solution.py:1096
  29.8 3.7 %captions_step.1 = (bf16[64,384]{1,0:T(8,128)(2,1)}, bf16[64,384]{1,0:T(8,128)(2,1)}, f32[8,384]{1,0:T(8,128)S(1)}, f32[16,384]{1,0:T(8,128)S(1)}, f32[16,384]{1...) custom-call(s32[3]{0:T(128)S(1)} %pad_add_fusion.where_ref, ...), custom_call_target="tpu_custom_call" | custom-call | flops 4000000000 | bytes 8000000 | tf_op jit(solution)/shard_map/captions_step/pallas_call | solution.py:521
  35.2 1.9 %collective-permute-start.7 = (f32[16,384]{1,0:T(8,128)S(1)}, f32[16,384]{1,0:T(8,128)S(1)}, u32[]{:S(2)}, u32[]{:S(2)}) collective-permute-start(f32[16,384]{1,0:T(8,128)S(1)} %get-tuple-element.155), channel_id=1, source_target_pairs={{0,4},{2,6},{4,0},{6,2},{1,5},{3,7},{5,1},{7,3},{8,12},{10,14},{12... | collective-permute-start | bytes 73736 | tf_op jit(solution)/shard_map/ppermute | solution.py:1096
  38.6 1.6 collective-permute-start.12
  40.3 1.9 %collective-permute-start.10 = (bf16[4,48,384]{2,1,0:T(8,128)(2,1)S(1)}, bf16[4,48,384]{2,1,0:T(8,128)(2,1)S(1)}, u32[]{:S(2)}, u32[]{:S(2)}) collective-permute-start(bf16[4,48,384]{2,1,0:T(8,128)(2,1)S(1)} %get-tuple-element.321.refs_0_), channel_id=1, source_target_pairs={{0,2},{2,0},{4,6},{6,4},{1,3},{3,1},{5,7},{7,5},{8,10},{10,8},{12,... | collective-permute-start | bytes 442376 | tf_op jit(solution)/shard_map/ppermute | solution.py:1096
  42.3 9.1 %attend.1 = (f32[10,208,384]{2,1,0:T(8,128)S(1)}, bf16[10,384,208]{2,1,0:T(8,128)(2,1)S(1)}, f32[10,8,208]{2,1,0:T(8,128)S(1)}) custom-call(bf16[10,208,384]{2,1,0:T(8,128)(2,1)S(1)} %copy-done.31, bf16[10,208,768]{2,1,0:T(8,128)(2,1)S(1)} %copy-done.29, bf16[10,197,384]{2,1,0:T(8,128)(2,1)S(1)} %bitcast.105, f32[16,384]{1,0:T(8,128)S(1)} %copy-done.39, ...), custom_call_target="tpu_custom_call" | custom-call | flops 14000000000 | bytes 10000000 | tf_op jit(solution)/shard_map/attend/pallas_call | solution.py:401
  51.6 1.6 collective-permute-start.13
  53.2 24.3 %mlp_step.1 = (bf16[10,197,384]{2,1,0:T(8,128)(2,1)S(1)}, f32[10,208,384]{2,1,0:T(8,128)S(1)}, f32[8,384]{1,0:T(8,128)S(1)}, bf16[4,4,48,768]{3,2,1,0:T(8,128)(2,1)S(1)}, bf16[4,4,48,768]{3,2,1,0:T(8,128)(2,1)S(1)}) custom-call(s32[3]{0:T(128)S(1)} %pad_add_fusion.where_ref, f32[10,208,384]{2,1,0:T(8,128)S(1)} %get-tuple-element.173.resid_ref, ...), custom_call_target="tpu_custom_call" | custom-call | flops 20000000000 | bytes 20000000 | tf_op jit(solution)/shard_map/mlp_step/pallas_call | solution.py:612
  77.7 2.3 %copy.44 = bf16[2,5,1,197,384]{4,0,3,2,1:T(2,128)(2,1)} copy(bf16[2,5,1,197,384]{4,3,1,0,2:T(8,128)(2,1)S(1)} %bitcast.111) | data formatting | bytes 3025920 | tf_op jit(solution)/shard_map/reshape | solution.py:1319
  80.8 2.6 %collective-permute-start.18 = (bf16[320,384]{1,0:T(8,128)(2,1)S(1)}, bf16[320,384]{1,0:T(8,128)(2,1)S(1)}, u32[]{:S(2)}, u32[]{:S(2)}) collective-permute-start(bf16[320,384]{1,0:T(8,128)(2,1)S(1)} %pad_maximum_fusion.2), channel_id=1, source_target_pairs={{0,16},{8,24},{16,0},{24,8},{1,17},{9,25},{17,1},{25,9},{2,18},{10... | collective-permute-start | bytes 737288 | tf_op jit(solution)/shard_map/ppermute | solution.py:1096
  84.0 1.5 collective-permute-start.16
  86.9 13.1 %attend_back.2 = (bf16[10,197,384]{2,1,0:T(8,128)(2,1)S(1)}, f32[16,384]{1,0:T(8,128)S(1)}, f32[16,384]{1,0:T(8,128)S(1)}, f32[8,384]{1,0:T(8,128)S(1)}, f32[1536,384]{1,0:T(8,128)S(1)}) custom-call(s32[3]{0:T(128)S(1)} %pad_add_fusion.where_ref, bf16[10,208,384]{2,1,0:T(8,128)(2,1)S(1)} %copy-done.31, bf16[10,208,768]{2,1,0:T(8,128)(2,1)S(1)} %copy-done.29, ...), custom_call_target="tpu_custom_call" | custom-call | flops 13500000256 | bytes 12000000 | tf_op jit(solution)/shard_map/attend_back/pallas_call | solution.py:752
  100.4 1.6 collective-permute-start.22
  104.4 9.9 %attend_back.3 = (bf16[10,197,384]{2,1,0:T(8,128)(2,1)S(1)}, f32[16,384]{1,0:T(8,128)S(1)}, f32[16,384]{1,0:T(8,128)S(1)}, f32[8,384]{1,0:T(8,128)S(1)}, bf16[4,...) custom-call(s32[3]{0:T(128)S(1)} %pad_add_fusion.where_ref, ...), custom_call_target="tpu_custom_call", output_to_operand_aliasing={{0}: (15, {})} | custom-call | flops 8999999488 | bytes 8000000 | tf_op jit(solution)/shard_map/attend_back/pallas_call | solution.py:752
  118.8 1.6 collective-permute-start.27
  120.6 1.8 collective-permute-start.25
  122.4 10.0 %collective-permute-done.23 = bf16[4,48,768]{2,1,0:T(8,128)(2,1)} collective-permute-done((bf16[4,48,768]{2,1,0:T(8,128)(2,1)S(1)}, bf16[4,48,768]{2,1,0:T(8,128)(2,1)}, u32[]{:S(2)}, u32[]{:S(2)}) %collective-permute-start.23) | collective-permute-done | bytes 294944 | tf_op jit(solution)/shard_map/ppermute | solution.py:1096
  135.5 1.5 collective-permute-start.31
  139.0 2.1 %collective-permute-done.32 = bf16[208,384]{1,0:T(8,128)(2,1)S(1)} collective-permute-done((bf16[208,384]{1,0:T(8,128)(2,1)S(1)}, bf16[208,384]{1,0:T(8,128)(2,1)S(1)}, u32[]{:S(2)}, u32[]{:S(2)}) %collective-permute-start.32) | collective-permute-done | bytes 159776 | tf_op jit(solution)/shard_map/ppermute | solution.py:1096
  141.8 5.4 %message_forward.1 = (bf16[1,512,384]{2,1,0:T(8,128)(2,1)}, bf16[1,512,384]{2,1,0:T(8,128)(2,1)}, bf16[1,512,384]{2,1,0:T(8,128)(2,1)}, bf16[1,384,512]{2,1,0:T(...) custom-call(s32[3]{0:T(128)} %copy-done.26, ...), custom_call_target="tpu_custom_call" | custom-call | flops 3000000000 | bytes 6000000 | tf_op jit(solution)/shard_map/message_forward/pallas_call | solution.py:911
  147.2 2.2 %unpack_side.1 = (f32[3,3,384,384]{3,2,1,0:T(8,128)}, f32[3,384,384]{2,1,0:T(8,128)}) custom-call(s32[3]{0:T(128)S(1)} %copy-done.27, bf16[4,4,48,384]{3,2,1,0:T(8,128)(2,1)S(1)} %pad_maximum_fusion.1.refs_0_, bf16[4,4,48,384]{3,2,1,0:T(8,128)(2,1)S(1)} %bitcast.112), custom_call_target="tpu_custom_call" | custom-call | flops 1000000000 | bytes 4000000 | tf_op jit(solution)/shard_map/unpack_side/pallas_call | solution.py:1226
  149.4 1.6 collective-permute-done.33
  153.7 1.5 collective-permute-start.34
  155.3 3.3 %unpack.1 = (f32[384,1536]{1,0:T(8,128)}, f32[1536,384]{1,0:T(8,128)}) custom-call(s32[3]{0:T(128)S(1)} %copy-done.27, bf16[16,48,768]{2,1,0:T(8,128)(2,1)S(1)} %constant_dynamic-update-slice_fusion.refs_0_, bf16[16,48,768]{2,1,0:T(8,128)(2,1)S(1)} %collective-permute-done.37.refs_1_), custom_call_target="tpu_custom_call" | custom-call | flops 2000000000 | bytes 10000000 | tf_op jit(solution)/shard_map/unpack/pallas_call | solution.py:1200
  158.5 1.8 %collective-permute-done.36.refs_3_ = bf16[256,384]{1,0:T(8,128)(2,1)S(1)} collective-permute-done((bf16[256,384]{1,0:T(8,128)(2,1)S(1)}, bf16[256,384]{1,0:T(8,128)(2,1)S(1)}, u32[]{:S(2)}, u32[]{:S(2)}) %collective-permute-start.36) | collective-permute-done | bytes 196640 | tf_op jit(solution)/shard_map/ppermute | solution.py:1096
  160.4 3.8 %collective-permute-done.35.refs_2_ = bf16[256,384]{1,0:T(8,128)(2,1)S(1)} collective-permute-done((bf16[256,384]{1,0:T(8,128)(2,1)S(1)}, bf16[256,384]{1,0:T(8,128)(2,1)S(1)}, u32[]{:S(2)}, u32[]{:S(2)}) %collective-permute-start.35) | collective-permute-done | bytes 196640 | tf_op jit(solution)/shard_map/ppermute | solution.py:1096
  166.9 7.4 %message_back.1 = (f32[3,3,384,384]{3,2,1,0:T(8,128)}, f32[3,384,384]{2,1,0:T(8,128)}, f32[384,384]{1,0:T(8,128)}, f32[384]{0:T(512)}, f32[4,384]{1,0:T(4,128)}, /*index=5*/f32[16,384]{1,0:T(8,128)S(1)}) custom-call(s32[3]{0:T(128)S(1)} %copy-done.27, ...), custom_call_target="tpu_custom_call", output_to_operand_aliasing={{0}: (20, {}), {1}: (21, {})} | custom-call | flops 4000000000 | bytes 12000000 | tf_op jit(solution)/shard_map/message_back/pallas_call | solution.py:1024
  (222 shorter events, 33.7 us)
Async XLA Ops:
  2.1 11.1 %collective-permute-start.2 = (bf16[16,384]{1,0:T(8,128)(2,1)}, bf16[16,384]{1,0:T(8,128)(2,1)S(1)}, u32[]{:S(2)}, u32[]{:S(2)}) collective-permute-start(bf16[16,384]{1,0:T(8,128)(2,1)} %class_rows.1.refs_0_), channel_id=1, source_target_pairs={{0,6},{2,4},{4,2},{6,0},{1,7},{3,5},{5,3},{7,1},{8,14},{10,12},{12... | collective-permute-start | bytes 36872 | tf_op jit(solution)/shard_map/ppermute | solution.py:1096
  6.0 7.2 %collective-permute-start.1 = (bf16[16,384]{1,0:T(8,128)(2,1)}, bf16[16,384]{1,0:T(8,128)(2,1)S(1)}, u32[]{:S(2)}, u32[]{:S(2)}) collective-permute-start(bf16[16,384]{1,0:T(8,128)(2,1)} %class_rows.1.refs_0_), channel_id=1, source_target_pairs={{0,4},{2,6},{4,0},{6,2},{1,5},{3,7},{5,1},{7,3},{8,12},{10,14},{12... | collective-permute-start | bytes 36872 | tf_op jit(solution)/shard_map/ppermute | solution.py:1096
  6.5 6.7 %collective-permute-start = (bf16[16,384]{1,0:T(8,128)(2,1)}, bf16[16,384]{1,0:T(8,128)(2,1)S(1)}, u32[]{:S(2)}, u32[]{:S(2)}) collective-permute-start(bf16[16,384]{1,0:T(8,128)(2,1)} %class_rows.1.refs_0_), channel_id=1, source_target_pairs={{0,2},{2,0},{4,6},{6,4},{1,3},{3,1},{5,7},{7,5},{8,10},{10,8},{12,... | collective-permute-start | bytes 36872 | tf_op jit(solution)/shard_map/ppermute | solution.py:1096
  21.8 4.8 %collective-permute-start.5 = (bf16[16,384]{1,0:T(8,128)(2,1)}, bf16[16,384]{1,0:T(8,128)(2,1)S(1)}, u32[]{:S(2)}, u32[]{:S(2)}) collective-permute-start(bf16[16,384]{1,0:T(8,128)(2,1)} %get-tuple-element.152.refs_0_), channel_id=1, source_target_pairs={{0,6},{2,4},{4,2},{6,0},{1,7},{3,5},{5,3},{7,1},{8,14},{10,12},{12... | collective-permute-start | bytes 36872 | tf_op jit(solution)/shard_map/ppermute | solution.py:1096
  35.0 5.3 %collective-permute-start.6 = (f32[16,384]{1,0:T(8,128)S(1)}, f32[16,384]{1,0:T(8,128)S(1)}, u32[]{:S(2)}, u32[]{:S(2)}) collective-permute-start(f32[16,384]{1,0:T(8,128)S(1)} %get-tuple-element.154), channel_id=1, source_target_pairs={{0,2},{2,0},{4,6},{6,4},{1,3},{3,1},{5,7},{7,5},{8,10},{10,8},{12,... | collective-permute-start | bytes 73736 | tf_op jit(solution)/shard_map/ppermute | solution.py:1096
  35.2 16.2 %collective-permute-start.7 = (f32[16,384]{1,0:T(8,128)S(1)}, f32[16,384]{1,0:T(8,128)S(1)}, u32[]{:S(2)}, u32[]{:S(2)}) collective-permute-start(f32[16,384]{1,0:T(8,128)S(1)} %get-tuple-element.155), channel_id=1, source_target_pairs={{0,4},{2,6},{4,0},{6,2},{1,5},{3,7},{5,1},{7,3},{8,12},{10,14},{12... | collective-permute-start | bytes 73736 | tf_op jit(solution)/shard_map/ppermute | solution.py:1096
  37.1 14.3 %collective-permute-start.8 = (f32[16,384]{1,0:T(8,128)S(1)}, f32[16,384]{1,0:T(8,128)S(1)}, u32[]{:S(2)}, u32[]{:S(2)}) collective-permute-start(f32[16,384]{1,0:T(8,128)S(1)} %get-tuple-element.156), channel_id=1, source_target_pairs={{0,6},{2,4},{4,2},{6,0},{1,7},{3,5},{5,3},{7,1},{8,14},{10,12},{12... | collective-permute-start | bytes 73736 | tf_op jit(solution)/shard_map/ppermute | solution.py:1096
  38.6 12.8 %collective-permute-start.12 = (bf16[4,48,384]{2,1,0:T(8,128)(2,1)S(1)}, bf16[4,48,384]{2,1,0:T(8,128)(2,1)S(1)}, u32[]{:S(2)}, u32[]{:S(2)}) collective-permute-start(bf16[4,48,384]{2,1,0:T(8,128)(2,1)S(1)} %get-tuple-element.319.refs_2_), channel_id=1, source_target_pairs={{0,6},{2,4},{4,2},{6,0},{1,7},{3,5},{5,3},{7,1},{8,14},{10,12},{12... | collective-permute-start | bytes 442376 | tf_op jit(solution)/shard_map/ppermute | solution.py:1096
  40.2 11.2 %collective-permute-start.11 = (bf16[4,48,384]{2,1,0:T(8,128)(2,1)S(1)}, bf16[4,48,384]{2,1,0:T(8,128)(2,1)S(1)}, u32[]{:S(2)}, u32[]{:S(2)}) collective-permute-start(bf16[4,48,384]{2,1,0:T(8,128)(2,1)S(1)} %get-tuple-element.320.refs_1_), channel_id=1, source_target_pairs={{0,4},{2,6},{4,0},{6,2},{1,5},{3,7},{5,1},{7,3},{8,12},{10,14},{12... | collective-permute-start | bytes 442376 | tf_op jit(solution)/shard_map/ppermute | solution.py:1096
  40.3 11.1 %collective-permute-start.10 = (bf16[4,48,384]{2,1,0:T(8,128)(2,1)S(1)}, bf16[4,48,384]{2,1,0:T(8,128)(2,1)S(1)}, u32[]{:S(2)}, u32[]{:S(2)}) collective-permute-start(bf16[4,48,384]{2,1,0:T(8,128)(2,1)S(1)} %get-tuple-element.321.refs_0_), channel_id=1, source_target_pairs={{0,2},{2,0},{4,6},{6,4},{1,3},{3,1},{5,7},{7,5},{8,10},{10,8},{12,... | collective-permute-start | bytes 442376 | tf_op jit(solution)/shard_map/ppermute | solution.py:1096
  51.6 26.0 %collective-permute-start.13 = (bf16[256,384]{1,0:T(8,128)(2,1)S(1)}, bf16[256,384]{1,0:T(8,128)(2,1)S(1)}, u32[]{:S(2)}, u32[]{:S(2)}) collective-permute-start(bf16[256,384]{1,0:T(8,128)(2,1)S(1)} %pad_maximum_fusion.3), channel_id=1, source_target_pairs={{0,8},{8,0},{16,24},{24,16},{1,9},{9,1},{17,25},{25,17},{2,10},{10... | collective-permute-start | bytes 589832 | tf_op jit(solution)/shard_map/ppermute | solution.py:1096
  80.8 19.2 %collective-permute-start.18 = (bf16[320,384]{1,0:T(8,128)(2,1)S(1)}, bf16[320,384]{1,0:T(8,128)(2,1)S(1)}, u32[]{:S(2)}, u32[]{:S(2)}) collective-permute-start(bf16[320,384]{1,0:T(8,128)(2,1)S(1)} %pad_maximum_fusion.2), channel_id=1, source_target_pairs={{0,16},{8,24},{16,0},{24,8},{1,17},{9,25},{17,1},{25,9},{2,18},{10... | collective-permute-start | bytes 737288 | tf_op jit(solution)/shard_map/ppermute | solution.py:1096
  83.4 16.7 %collective-permute-start.15 = (bf16[4,48,768]{2,1,0:T(8,128)(2,1)S(1)}, bf16[4,48,768]{2,1,0:T(8,128)(2,1)S(1)}, u32[]{:S(2)}, u32[]{:S(2)}) collective-permute-start(bf16[4,48,768]{2,1,0:T(8,128)(2,1)S(1)} %get-tuple-element.202), channel_id=1, source_target_pairs={{0,2},{2,0},{4,6},{6,4},{1,3},{3,1},{5,7},{7,5},{8,10},{10,8},{12,... | collective-permute-start | bytes 884744 | tf_op jit(solution)/shard_map/ppermute | solution.py:1096
  84.0 16.2 %collective-permute-start.16 = (bf16[4,48,768]{2,1,0:T(8,128)(2,1)S(1)}, bf16[4,48,768]{2,1,0:T(8,128)(2,1)S(1)}, u32[]{:S(2)}, u32[]{:S(2)}) collective-permute-start(bf16[4,48,768]{2,1,0:T(8,128)(2,1)S(1)} %get-tuple-element.203), channel_id=1, source_target_pairs={{0,4},{2,6},{4,0},{6,2},{1,5},{3,7},{5,1},{7,3},{8,12},{10,14},{12... | collective-permute-start | bytes 884744 | tf_op jit(solution)/shard_map/ppermute | solution.py:1096
  85.5 14.7 %collective-permute-start.17 = (bf16[4,48,768]{2,1,0:T(8,128)(2,1)S(1)}, bf16[4,48,768]{2,1,0:T(8,128)(2,1)S(1)}, u32[]{:S(2)}, u32[]{:S(2)}) collective-permute-start(bf16[4,48,768]{2,1,0:T(8,128)(2,1)S(1)} %get-tuple-element.204), channel_id=1, source_target_pairs={{0,6},{2,4},{4,2},{6,0},{1,7},{3,5},{5,3},{7,1},{8,14},{10,12},{12... | collective-permute-start | bytes 884744 | tf_op jit(solution)/shard_map/ppermute | solution.py:1096
  100.4 14.0 %collective-permute-start.22 = (bf16[4,48,384]{2,1,0:T(8,128)(2,1)S(1)}, bf16[4,48,384]{2,1,0:T(8,128)(2,1)S(1)}, u32[]{:S(2)}, u32[]{:S(2)}) collective-permute-start(bf16[4,48,384]{2,1,0:T(8,128)(2,1)S(1)} %fusion.8), channel_id=1, source_target_pairs={{0,6},{2,4},{4,2},{6,0},{1,7},{3,5},{5,3},{7,1},{8,14},{10,12},{12... | collective-permute-start | bytes 442376 | tf_op jit(solution)/shard_map/ppermute | solution.py:1096
  101.9 12.4 %collective-permute-start.21 = (bf16[4,48,384]{2,1,0:T(8,128)(2,1)S(1)}, bf16[4,48,384]{2,1,0:T(8,128)(2,1)S(1)}, u32[]{:S(2)}, u32[]{:S(2)}) collective-permute-start(bf16[4,48,384]{2,1,0:T(8,128)(2,1)S(1)} %fusion.8), channel_id=1, source_target_pairs={{0,4},{2,6},{4,0},{6,2},{1,5},{3,7},{5,1},{7,3},{8,12},{10,14},{12... | collective-permute-start | bytes 442376 | tf_op jit(solution)/shard_map/ppermute | solution.py:1096
  102.5 11.9 %collective-permute-start.20 = (bf16[4,48,384]{2,1,0:T(8,128)(2,1)S(1)}, bf16[4,48,384]{2,1,0:T(8,128)(2,1)S(1)}, u32[]{:S(2)}, u32[]{:S(2)}) collective-permute-start(bf16[4,48,384]{2,1,0:T(8,128)(2,1)S(1)} %fusion.8), channel_id=1, source_target_pairs={{0,2},{2,0},{4,6},{6,4},{1,3},{3,1},{5,7},{7,5},{8,10},{10,8},{12,... | collective-permute-start | bytes 442376 | tf_op jit(solution)/shard_map/ppermute | solution.py:1096
  103.9 10.3 %collective-permute-start.19 = (bf16[4,48,768]{2,1,0:T(8,128)(2,1)S(1)}, bf16[4,48,768]{2,1,0:T(8,128)(2,1)S(1)}, u32[]{:S(2)}, u32[]{:S(2)}) collective-permute-start(bf16[4,48,768]{2,1,0:T(8,128)(2,1)S(1)} %fusion.2), channel_id=1, source_target_pairs={{0,8},{8,0},{16,24},{24,16},{1,9},{9,1},{17,25},{25,17},{2,10},{10... | collective-permute-start | bytes 884744 | tf_op jit(solution)/shard_map/ppermute | solution.py:1096
  115.6 17.9 %collective-permute-start.28 = (bf16[1024,384]{1,0:T(8,128)(2,1)S(1)}, bf16[1024,384]{1,0:T(8,128)(2,1)S(1)}, u32[]{:S(2)}, u32[]{:S(2)}) collective-permute-start(bf16[1024,384]{1,0:T(8,128)(2,1)S(1)} %pad_maximum_fusion), channel_id=1, source_target_pairs={{0,1},{1,0},{2,3},{3,2},{4,5},{5,4},{6,7},{7,6},{8,9},{9,8},{10,11... | collective-permute-start | bytes 2359304 | tf_op jit(solution)/shard_map/ppermute | solution.py:1096
  115.7 16.7 %collective-permute-start.23 = (bf16[4,48,768]{2,1,0:T(8,128)(2,1)S(1)}, bf16[4,48,768]{2,1,0:T(8,128)(2,1)}, u32[]{:S(2)}, u32[]{:S(2)}) collective-permute-start(bf16[4,48,768]{2,1,0:T(8,128)(2,1)S(1)} %add_convert_fusion.1), channel_id=1, source_target_pairs={{0,16},{8,24},{16,0},{24,8},{1,17},{9,25},{17,1},{25,9},{2,18},{10... | collective-permute-start | bytes 884744 | tf_op jit(solution)/shard_map/ppermute | solution.py:1096
  118.8 15.4 %collective-permute-start.27 = (bf16[4,48,384]{2,1,0:T(8,128)(2,1)S(1)}, bf16[4,48,384]{2,1,0:T(8,128)(2,1)S(1)}, u32[]{:S(2)}, u32[]{:S(2)}) collective-permute-start(bf16[4,48,384]{2,1,0:T(8,128)(2,1)S(1)} %get-tuple-element.316), channel_id=1, source_target_pairs={{0,6},{2,4},{4,2},{6,0},{1,7},{3,5},{5,3},{7,1},{8,14},{10,12},{12... | collective-permute-start | bytes 442376 | tf_op jit(solution)/shard_map/ppermute | solution.py:1096
  120.4 13.9 %collective-permute-start.26 = (bf16[4,48,384]{2,1,0:T(8,128)(2,1)S(1)}, bf16[4,48,384]{2,1,0:T(8,128)(2,1)S(1)}, u32[]{:S(2)}, u32[]{:S(2)}) collective-permute-start(bf16[4,48,384]{2,1,0:T(8,128)(2,1)S(1)} %get-tuple-element.317), channel_id=1, source_target_pairs={{0,4},{2,6},{4,0},{6,2},{1,5},{3,7},{5,1},{7,3},{8,12},{10,14},{12... | collective-permute-start | bytes 442376 | tf_op jit(solution)/shard_map/ppermute | solution.py:1096
  120.6 13.6 %collective-permute-start.25 = (bf16[4,48,384]{2,1,0:T(8,128)(2,1)S(1)}, bf16[4,48,384]{2,1,0:T(8,128)(2,1)S(1)}, u32[]{:S(2)}, u32[]{:S(2)}) collective-permute-start(bf16[4,48,384]{2,1,0:T(8,128)(2,1)S(1)} %get-tuple-element.318), channel_id=1, source_target_pairs={{0,2},{2,0},{4,6},{6,4},{1,3},{3,1},{5,7},{7,5},{8,10},{10,8},{12,... | collective-permute-start | bytes 442376 | tf_op jit(solution)/shard_map/ppermute | solution.py:1096
  135.4 5.7 %collective-permute-start.32 = (bf16[208,384]{1,0:T(8,128)(2,1)S(1)}, bf16[208,384]{1,0:T(8,128)(2,1)S(1)}, u32[]{:S(2)}, u32[]{:S(2)}) collective-permute-start(bf16[208,384]{1,0:T(8,128)(2,1)S(1)} %pad_maximum_fusion.7), channel_id=1, source_target_pairs={{0,8},{8,0},{16,24},{24,16},{1,9},{9,1},{17,25},{25,17},{2,10},{10... | collective-permute-start | bytes 479240 | tf_op jit(solution)/shard_map/ppermute | solution.py:1096
  135.5 15.6 %collective-permute-start.31 = (bf16[4,48,768]{2,1,0:T(8,128)(2,1)S(1)}, bf16[4,48,768]{2,1,0:T(8,128)(2,1)S(1)}, u32[]{:S(2)}, u32[]{:S(2)}) collective-permute-start(bf16[4,48,768]{2,1,0:T(8,128)(2,1)S(1)} %add_convert_fusion), channel_id=1, source_target_pairs={{0,6},{2,4},{4,2},{6,0},{1,7},{3,5},{5,3},{7,1},{8,14},{10,12},{12... | collective-permute-start | bytes 884744 | tf_op jit(solution)/shard_map/ppermute | solution.py:1096
  137.0 14.3 %collective-permute-start.30 = (bf16[4,48,768]{2,1,0:T(8,128)(2,1)S(1)}, bf16[4,48,768]{2,1,0:T(8,128)(2,1)S(1)}, u32[]{:S(2)}, u32[]{:S(2)}) collective-permute-start(bf16[4,48,768]{2,1,0:T(8,128)(2,1)S(1)} %add_convert_fusion), channel_id=1, source_target_pairs={{0,4},{2,6},{4,0},{6,2},{1,5},{3,7},{5,1},{7,3},{8,12},{10,14},{12... | collective-permute-start | bytes 884744 | tf_op jit(solution)/shard_map/ppermute | solution.py:1096
  137.5 13.9 %collective-permute-start.29 = (bf16[4,48,768]{2,1,0:T(8,128)(2,1)S(1)}, bf16[4,48,768]{2,1,0:T(8,128)(2,1)S(1)}, u32[]{:S(2)}, u32[]{:S(2)}) collective-permute-start(bf16[4,48,768]{2,1,0:T(8,128)(2,1)S(1)} %add_convert_fusion), channel_id=1, source_target_pairs={{0,2},{2,0},{4,6},{6,4},{1,3},{3,1},{5,7},{7,5},{8,10},{10,8},{12,... | collective-permute-start | bytes 884744 | tf_op jit(solution)/shard_map/ppermute | solution.py:1096
  141.3 9.7 %collective-permute-start.33 = (bf16[224,384]{1,0:T(8,128)(2,1)S(1)}, bf16[224,384]{1,0:T(8,128)(2,1)S(1)}, u32[]{:S(2)}, u32[]{:S(2)}) collective-permute-start(bf16[224,384]{1,0:T(8,128)(2,1)S(1)} %pad_maximum_fusion.6), channel_id=1, source_target_pairs={{0,16},{8,24},{16,0},{24,8},{1,17},{9,25},{17,1},{25,9},{2,18},{10... | collective-permute-start | bytes 516104 | tf_op jit(solution)/shard_map/ppermute | solution.py:1096
  151.6 8.7 %collective-permute-start.36 = (bf16[256,384]{1,0:T(8,128)(2,1)S(1)}, bf16[256,384]{1,0:T(8,128)(2,1)S(1)}, u32[]{:S(2)}, u32[]{:S(2)}) collective-permute-start(bf16[256,384]{1,0:T(8,128)(2,1)S(1)} %pad_maximum_fusion.5.refs_0_), channel_id=1, source_target_pairs={{0,6},{2,4},{4,2},{6,0},{1,7},{3,5},{5,3},{7,1},{8,14},{10,12},{12... | collective-permute-start | bytes 589832 | tf_op jit(solution)/shard_map/ppermute | solution.py:1096
  153.1 11.0 %collective-permute-start.35 = (bf16[256,384]{1,0:T(8,128)(2,1)S(1)}, bf16[256,384]{1,0:T(8,128)(2,1)S(1)}, u32[]{:S(2)}, u32[]{:S(2)}) collective-permute-start(bf16[256,384]{1,0:T(8,128)(2,1)S(1)} %pad_maximum_fusion.5.refs_0_), channel_id=1, source_target_pairs={{0,4},{2,6},{4,0},{6,2},{1,5},{3,7},{5,1},{7,3},{8,12},{10,14},{12... | collective-permute-start | bytes 589832 | tf_op jit(solution)/shard_map/ppermute | solution.py:1096
  153.7 10.4 %collective-permute-start.34 = (bf16[256,384]{1,0:T(8,128)(2,1)S(1)}, bf16[256,384]{1,0:T(8,128)(2,1)S(1)}, u32[]{:S(2)}, u32[]{:S(2)}) collective-permute-start(bf16[256,384]{1,0:T(8,128)(2,1)S(1)} %pad_maximum_fusion.5.refs_0_), channel_id=1, source_target_pairs={{0,2},{2,0},{4,6},{6,4},{1,3},{3,1},{5,7},{7,5},{8,10},{10,8},{12,... | collective-permute-start | bytes 589832 | tf_op jit(solution)/shard_map/ppermute | solution.py:1096
  (65 other events, 473.1 us)

commit v2 on v1

--- a/solution.py
+++ b/solution.py
@@ -921,7 +921,7 @@
         out_specs=[full(x.shape) for x in outs],
         out_shape=outs,
         scratch_shapes=[pltpu.VMEM((width, width), bf16)] * 3,
-        compiler_params=params(56),
+        compiler_params=params(48 if steps == 1 else 56),
         cost_estimate=cost(3e9, 6e6),
         name="message_forward",
     )(where, *side, mw, mg, qkv)

time: 176 us -> 176 us (level)
    unnamed x115 -> x99, local copies, waits for them, and re-layouts: 8.27 us -> 8.25 us
  transfers between devices with their start and end apart: 42 -> 42, of which waited for: 11 -> 12; matrix products, arithmetic and copies ran while one was open for 5% -> 4% of each run, Pallas kernels for 41% -> 40%
where the time goes in v2:
time: 176 us; the launch traced here: 175 us
  Pallas kernels  90.8 us (52%)
  starting transfers between devices  40 us (23%)
  waiting for transfers between devices  25.5 us (14%)
  local copies, waits for them, and re-layouts  12.5 us (7%)
  other arithmetic  4.85 us (3%)
    ppermute x42, starting transfers between devices, swap(): return lax.ppermute(x, axis, [(i, i ^ k) for i in range(count)])  40 us
    ppermute x42, waiting for transfers between devices, swap(): return lax.ppermute(x, axis, [(i, i ^ k) for i in range(count)])  25.5 us
    pallas_call x1, Pallas kernels, mlp_step(): pl.pallas_call(functools.partial(mlp_kernel, len(parts), patch, ff), grid...  24.5 us
    pallas_call x2, Pallas kernels, attend_back(): pl.pallas_call(functools.partial(attend_back_kernel, patch + 1, first, la...  22.9 us
    pallas_call x1, Pallas kernels, attend(): pl.pallas_call(functools.partial(attend_kernel, tokens), grid=(count // b...  9.12 us
    unnamed x99, local copies, waits for them, and re-layouts  8.25 us
    pallas_call x1, Pallas kernels, first_rows(): pl.pallas_call(functools.partial(first_kernel, len(gathered), count, toke...  7.99 us
    pallas_call x1, Pallas kernels, message_back(): pl.pallas_call(functools.partial(message_back_kernel, layout, groups), gr...  7.4 us
  transfers between devices with their start and end apart: 42, of which 12 were waited for; matrix products, arithmetic and copies ran while one was open for 4% of the time, Pallas kernels for 40%

profile of v2, /device:TPU:0, one launch (start us, length us, event | category | flops | bytes accessed | tf_op | source)
XLA Modules:
  0.0 175.2 jit_solution(15944198770917429515)
XLA Ops:
  2.1 3.9 %collective-permute-start.2 = (bf16[16,384]{1,0:T(8,128)(2,1)}, bf16[16,384]{1,0:T(8,128)(2,1)S(1)}, u32[]{:S(2)}, u32[]{:S(2)}) collective-permute-start(bf16[16,384]{1,0:T(8,128)(2,1)} %class_rows.1.refs_0_), channel_id=1, source_target_pairs={{0,6},{2,4},{4,2},{6,0},{1,7},{3,5},{5,3},{7,1},{8,14},{10,12},{12... | collective-permute-start | bytes 36872 | tf_op jit(solution)/shard_map/ppermute | solution.py:1096
  6.9 2.9 %norm_tokens.1 = (bf16[10,208,384]{2,1,0:T(8,128)(2,1)S(1)}, bf16[10,208,768]{2,1,0:T(8,128)(2,1)S(1)}) custom-call(bf16[10,197,384]{2,1,0:T(8,128)(2,1)S(1)} %bitcast.104, f32[4,384]{1,0:T(4,128)S(1)} %copy-done.18, bf16[3,3,384,384]{3,2,1,0:T(8,128)(2,1)S(1)} %copy-done, bf16[3,3,384,384]{3,2,1,0:T(8,128)(2,1)S(1)} %copy-done), custom_call_target="tpu_custom_call" | custom-call | flops 1226833920 | bytes 6389760 | tf_op jit(solution)/shard_map/norm_tokens/pallas_call | solution.py:178
  9.8 1.7 copy-done.21
  13.8 8.0 %first_rows.1 = (f32[16,384]{1,0:T(8,128)}, f32[16,384]{1,0:T(8,128)}, f32[16,768]{1,0:T(8,128)}, bf16[16,384]{1,0:T(8,128)(2,1)}, f32[16,384]{1,0:T(8,128)}) custom-call(bf16[16,384]{1,0:T(8,128)(2,1)} %class_rows.1.refs_0_, bf16[16,384]{1,0:T(8,128)(2,1)} %copy-done.44, bf16[16,384]{1,0:T(8,128)(2,1)} %copy-done.42, bf16[16,384]{1,0:T(8,128)(2,1)} %copy-done.40, ...), custom_call_target="tpu_custom_call" | custom-call | flops 4000000000 | bytes 12000000 | tf_op jit(solution)/shard_map/first_rows/pallas_call | solution.py:286
  21.8 2.9 %collective-permute-start.5 = (bf16[16,384]{1,0:T(8,128)(2,1)}, bf16[16,384]{1,0:T(8,128)(2,1)S(1)}, u32[]{:S(2)}, u32[]{:S(2)}) collective-permute-start(bf16[16,384]{1,0:T(8,128)(2,1)} %get-tuple-element.152.refs_0_), channel_id=1, source_target_pairs={{0,6},{2,4},{4,2},{6,0},{1,7},{3,5},{5,3},{7,1},{8,14},{10,12},{12... | collective-permute-start | bytes 36872 | tf_op jit(solution)/shard_map/ppermute | solution.py:1096
  26.6 2.0 %collective-permute-done.4.refs_2_ = bf16[16,384]{1,0:T(8,128)(2,1)S(1)} collective-permute-done((bf16[16,384]{1,0:T(8,128)(2,1)}, bf16[16,384]{1,0:T(8,128)(2,1)S(1)}, u32[]{:S(2)}, u32[]{:S(2)}) %collective-permute-start.4) | collective-permute-done | bytes 12320 | tf_op jit(solution)/shard_map/ppermute | solution.py:1096
  29.8 3.8 %captions_step.1 = (bf16[64,384]{1,0:T(8,128)(2,1)}, bf16[64,384]{1,0:T(8,128)(2,1)}, f32[8,384]{1,0:T(8,128)S(1)}, f32[16,384]{1,0:T(8,128)S(1)}, f32[16,384]{1...) custom-call(s32[3]{0:T(128)S(1)} %pad_add_fusion.where_ref, ...), custom_call_target="tpu_custom_call" | custom-call | flops 4000000000 | bytes 8000000 | tf_op jit(solution)/shard_map/captions_step/pallas_call | solution.py:521
  35.2 1.9 %collective-permute-start.7 = (f32[16,384]{1,0:T(8,128)S(1)}, f32[16,384]{1,0:T(8,128)S(1)}, u32[]{:S(2)}, u32[]{:S(2)}) collective-permute-start(f32[16,384]{1,0:T(8,128)S(1)} %get-tuple-element.155), channel_id=1, source_target_pairs={{0,4},{2,6},{4,0},{6,2},{1,5},{3,7},{5,1},{7,3},{8,12},{10,14},{12... | collective-permute-start | bytes 73736 | tf_op jit(solution)/shard_map/ppermute | solution.py:1096
  38.6 1.6 collective-permute-start.12
  40.3 1.9 %collective-permute-start.10 = (bf16[4,48,384]{2,1,0:T(8,128)(2,1)S(1)}, bf16[4,48,384]{2,1,0:T(8,128)(2,1)S(1)}, u32[]{:S(2)}, u32[]{:S(2)}) collective-permute-start(bf16[4,48,384]{2,1,0:T(8,128)(2,1)S(1)} %get-tuple-element.321.refs_0_), channel_id=1, source_target_pairs={{0,2},{2,0},{4,6},{6,4},{1,3},{3,1},{5,7},{7,5},{8,10},{10,8},{12,... | collective-permute-start | bytes 442376 | tf_op jit(solution)/shard_map/ppermute | solution.py:1096
  42.3 9.1 %attend.1 = (f32[10,208,384]{2,1,0:T(8,128)S(1)}, bf16[10,384,208]{2,1,0:T(8,128)(2,1)S(1)}, f32[10,8,208]{2,1,0:T(8,128)S(1)}) custom-call(bf16[10,208,384]{2,1,0:T(8,128)(2,1)S(1)} %copy-done.24, bf16[10,208,768]{2,1,0:T(8,128)(2,1)S(1)} %copy-done.22, bf16[10,197,384]{2,1,0:T(8,128)(2,1)S(1)} %bitcast.105, f32[16,384]{1,0:T(8,128)S(1)} %copy-done.32, ...), custom_call_target="tpu_custom_call" | custom-call | flops 14000000000 | bytes 10000000 | tf_op jit(solution)/shard_map/attend/pallas_call | solution.py:401
  51.6 1.6 collective-permute-start.13
  53.2 24.5 %mlp_step.1 = (bf16[10,197,384]{2,1,0:T(8,128)(2,1)S(1)}, f32[10,208,384]{2,1,0:T(8,128)S(1)}, f32[8,384]{1,0:T(8,128)S(1)}, bf16[4,4,48,768]{3,2,1,0:T(8,128)(2,1)S(1)}, bf16[4,4,48,768]{3,2,1,0:T(8,128)(2,1)S(1)}) custom-call(s32[3]{0:T(128)S(1)} %pad_add_fusion.where_ref, f32[10,208,384]{2,1,0:T(8,128)S(1)} %get-tuple-element.173.resid_ref, ...), custom_call_target="tpu_custom_call" | custom-call | flops 20000000000 | bytes 20000000 | tf_op jit(solution)/shard_map/mlp_step/pallas_call | solution.py:612
  78.0 2.3 %copy.44 = bf16[2,5,1,197,384]{4,0,3,2,1:T(2,128)(2,1)} copy(bf16[2,5,1,197,384]{4,3,1,0,2:T(8,128)(2,1)S(1)} %bitcast.111) | data formatting | bytes 3025920 | tf_op jit(solution)/shard_map/reshape | solution.py:1319
  81.0 2.6 %collective-permute-start.18 = (bf16[320,384]{1,0:T(8,128)(2,1)S(1)}, bf16[320,384]{1,0:T(8,128)(2,1)S(1)}, u32[]{:S(2)}, u32[]{:S(2)}) collective-permute-start(bf16[320,384]{1,0:T(8,128)(2,1)S(1)} %pad_maximum_fusion.2), channel_id=1, source_target_pairs={{0,16},{8,24},{16,0},{24,8},{1,17},{9,25},{17,1},{25,9},{2,18},{10... | collective-permute-start | bytes 737288 | tf_op jit(solution)/shard_map/ppermute | solution.py:1096
  84.2 1.5 collective-permute-start.16
  87.2 13.1 %attend_back.2 = (bf16[10,197,384]{2,1,0:T(8,128)(2,1)S(1)}, f32[16,384]{1,0:T(8,128)S(1)}, f32[16,384]{1,0:T(8,128)S(1)}, f32[8,384]{1,0:T(8,128)S(1)}, f32[1536,384]{1,0:T(8,128)S(1)}) custom-call(s32[3]{0:T(128)S(1)} %pad_add_fusion.where_ref, bf16[10,208,384]{2,1,0:T(8,128)(2,1)S(1)} %copy-done.24, bf16[10,208,768]{2,1,0:T(8,128)(2,1)S(1)} %copy-done.22, ...), custom_call_target="tpu_custom_call" | custom-call | flops 13500000256 | bytes 12000000 | tf_op jit(solution)/shard_map/attend_back/pallas_call | solution.py:752
  100.7 1.6 collective-permute-start.22
  104.7 9.9 %attend_back.3 = (bf16[10,197,384]{2,1,0:T(8,128)(2,1)S(1)}, f32[16,384]{1,0:T(8,128)S(1)}, f32[16,384]{1,0:T(8,128)S(1)}, f32[8,384]{1,0:T(8,128)S(1)}, bf16[4,...) custom-call(s32[3]{0:T(128)S(1)} %pad_add_fusion.where_ref, ...), custom_call_target="tpu_custom_call", output_to_operand_aliasing={{0}: (15, {})} | custom-call | flops 8999999488 | bytes 8000000 | tf_op jit(solution)/shard_map/attend_back/pallas_call | solution.py:752
  119.1 1.5 collective-permute-start.27
  120.9 1.7 collective-permute-start.25
  122.7 10.0 %collective-permute-done.23 = bf16[4,48,768]{2,1,0:T(8,128)(2,1)} collective-permute-done((bf16[4,48,768]{2,1,0:T(8,128)(2,1)S(1)}, bf16[4,48,768]{2,1,0:T(8,128)(2,1)}, u32[]{:S(2)}, u32[]{:S(2)}) %collective-permute-start.23) | collective-permute-done | bytes 294944 | tf_op jit(solution)/shard_map/ppermute | solution.py:1096
  135.2 1.6 collective-permute-start.31
  138.7 2.1 %collective-permute-done.32 = bf16[208,384]{1,0:T(8,128)(2,1)S(1)} collective-permute-done((bf16[208,384]{1,0:T(8,128)(2,1)S(1)}, bf16[208,384]{1,0:T(8,128)(2,1)S(1)}, u32[]{:S(2)}, u32[]{:S(2)}) %collective-permute-start.32) | collective-permute-done | bytes 159776 | tf_op jit(solution)/shard_map/ppermute | solution.py:1096
  141.5 4.0 %message_forward.1 = (bf16[1,512,384]{2,1,0:T(8,128)(2,1)S(1)}, bf16[1,512,384]{2,1,0:T(8,128)(2,1)S(1)}, bf16[1,512,384]{2,1,0:T(8,128)(2,1)S(1)}, bf16[1,384,5...) custom-call(s32[3]{0:T(128)S(1)} %pad_add_fusion.where_ref, ...), custom_call_target="tpu_custom_call" | custom-call | flops 3000000000 | bytes 6000000 | tf_op jit(solution)/shard_map/message_forward/pallas_call | solution.py:911
  145.5 2.2 %unpack_side.1 = (f32[3,3,384,384]{3,2,1,0:T(8,128)}, f32[3,384,384]{2,1,0:T(8,128)}) custom-call(s32[3]{0:T(128)S(1)} %pad_add_fusion.where_ref, bf16[4,4,48,384]{3,2,1,0:T(8,128)(2,1)S(1)} %pad_maximum_fusion.1.refs_0_, bf16[4,4,48,384]{3,2,1,0:T(8,128)(2,1)S(1)} %bitcast.113), custom_call_target="tpu_custom_call" | custom-call | flops 1000000000 | bytes 4000000 | tf_op jit(solution)/shard_map/unpack_side/pallas_call | solution.py:1226
  147.6 3.0 %collective-permute-done.33 = bf16[224,384]{1,0:T(8,128)(2,1)S(1)} collective-permute-done((bf16[224,384]{1,0:T(8,128)(2,1)S(1)}, bf16[224,384]{1,0:T(8,128)(2,1)S(1)}, u32[]{:S(2)}, u32[]{:S(2)}) %collective-permute-start.33) | collective-permute-done | bytes 172064 | tf_op jit(solution)/shard_map/ppermute | solution.py:1096
  153.4 1.5 collective-permute-start.34
  154.9 3.3 %unpack.1 = (f32[384,1536]{1,0:T(8,128)}, f32[1536,384]{1,0:T(8,128)}) custom-call(s32[3]{0:T(128)S(1)} %pad_add_fusion.where_ref, bf16[16,48,768]{2,1,0:T(8,128)(2,1)S(1)} %constant_dynamic-update-slice_fusion.refs_0_, bf16[16,48,768]{2,1,0:T(8,128)(2,1)S(1)} %collective-permute-done.37.refs_1_), custom_call_target="tpu_custom_call" | custom-call | flops 2000000000 | bytes 10000000 | tf_op jit(solution)/shard_map/unpack/pallas_call | solution.py:1200
  158.2 1.9 %collective-permute-done.36.refs_3_ = bf16[256,384]{1,0:T(8,128)(2,1)S(1)} collective-permute-done((bf16[256,384]{1,0:T(8,128)(2,1)S(1)}, bf16[256,384]{1,0:T(8,128)(2,1)S(1)}, u32[]{:S(2)}, u32[]{:S(2)}) %collective-permute-start.36) | collective-permute-done | bytes 196640 | tf_op jit(solution)/shard_map/ppermute | solution.py:1096
  160.1 3.8 %collective-permute-done.35.refs_2_ = bf16[256,384]{1,0:T(8,128)(2,1)S(1)} collective-permute-done((bf16[256,384]{1,0:T(8,128)(2,1)S(1)}, bf16[256,384]{1,0:T(8,128)(2,1)S(1)}, u32[]{:S(2)}, u32[]{:S(2)}) %collective-permute-start.35) | collective-permute-done | bytes 196640 | tf_op jit(solution)/shard_map/ppermute | solution.py:1096
  166.6 7.4 %message_back.1 = (f32[3,3,384,384]{3,2,1,0:T(8,128)}, f32[3,384,384]{2,1,0:T(8,128)}, f32[384,384]{1,0:T(8,128)}, f32[384]{0:T(512)}, f32[4,384]{1,0:T(4,128)}, /*index=5*/f32[16,384]{1,0:T(8,128)S(1)}) custom-call(s32[3]{0:T(128)S(1)} %pad_add_fusion.where_ref, ...), custom_call_target="tpu_custom_call", output_to_operand_aliasing={{0}: (20, {}), {1}: (21, {})} | custom-call | flops 4000000000 | bytes 12000000 | tf_op jit(solution)/shard_map/message_back/pallas_call | solution.py:1024
  (206 shorter events, 33.1 us)
Async XLA Ops:
  2.1 11.1 %collective-permute-start.2 = (bf16[16,384]{1,0:T(8,128)(2,1)}, bf16[16,384]{1,0:T(8,128)(2,1)S(1)}, u32[]{:S(2)}, u32[]{:S(2)}) collective-permute-start(bf16[16,384]{1,0:T(8,128)(2,1)} %class_rows.1.refs_0_), channel_id=1, source_target_pairs={{0,6},{2,4},{4,2},{6,0},{1,7},{3,5},{5,3},{7,1},{8,14},{10,12},{12... | collective-permute-start | bytes 36872 | tf_op jit(solution)/shard_map/ppermute | solution.py:1096
  6.0 7.2 %collective-permute-start.1 = (bf16[16,384]{1,0:T(8,128)(2,1)}, bf16[16,384]{1,0:T(8,128)(2,1)S(1)}, u32[]{:S(2)}, u32[]{:S(2)}) collective-permute-start(bf16[16,384]{1,0:T(8,128)(2,1)} %class_rows.1.refs_0_), channel_id=1, source_target_pairs={{0,4},{2,6},{4,0},{6,2},{1,5},{3,7},{5,1},{7,3},{8,12},{10,14},{12... | collective-permute-start | bytes 36872 | tf_op jit(solution)/shard_map/ppermute | solution.py:1096
  6.5 6.7 %collective-permute-start = (bf16[16,384]{1,0:T(8,128)(2,1)}, bf16[16,384]{1,0:T(8,128)(2,1)S(1)}, u32[]{:S(2)}, u32[]{:S(2)}) collective-permute-start(bf16[16,384]{1,0:T(8,128)(2,1)} %class_rows.1.refs_0_), channel_id=1, source_target_pairs={{0,2},{2,0},{4,6},{6,4},{1,3},{3,1},{5,7},{7,5},{8,10},{10,8},{12,... | collective-permute-start | bytes 36872 | tf_op jit(solution)/shard_map/ppermute | solution.py:1096
  21.8 4.8 %collective-permute-start.5 = (bf16[16,384]{1,0:T(8,128)(2,1)}, bf16[16,384]{1,0:T(8,128)(2,1)S(1)}, u32[]{:S(2)}, u32[]{:S(2)}) collective-permute-start(bf16[16,384]{1,0:T(8,128)(2,1)} %get-tuple-element.152.refs_0_), channel_id=1, source_target_pairs={{0,6},{2,4},{4,2},{6,0},{1,7},{3,5},{5,3},{7,1},{8,14},{10,12},{12... | collective-permute-start | bytes 36872 | tf_op jit(solution)/shard_map/ppermute | solution.py:1096
  35.0 5.3 %collective-permute-start.6 = (f32[16,384]{1,0:T(8,128)S(1)}, f32[16,384]{1,0:T(8,128)S(1)}, u32[]{:S(2)}, u32[]{:S(2)}) collective-permute-start(f32[16,384]{1,0:T(8,128)S(1)} %get-tuple-element.154), channel_id=1, source_target_pairs={{0,2},{2,0},{4,6},{6,4},{1,3},{3,1},{5,7},{7,5},{8,10},{10,8},{12,... | collective-permute-start | bytes 73736 | tf_op jit(solution)/shard_map/ppermute | solution.py:1096
  35.2 16.2 %collective-permute-start.7 = (f32[16,384]{1,0:T(8,128)S(1)}, f32[16,384]{1,0:T(8,128)S(1)}, u32[]{:S(2)}, u32[]{:S(2)}) collective-permute-start(f32[16,384]{1,0:T(8,128)S(1)} %get-tuple-element.155), channel_id=1, source_target_pairs={{0,4},{2,6},{4,0},{6,2},{1,5},{3,7},{5,1},{7,3},{8,12},{10,14},{12... | collective-permute-start | bytes 73736 | tf_op jit(solution)/shard_map/ppermute | solution.py:1096
  37.1 14.3 %collective-permute-start.8 = (f32[16,384]{1,0:T(8,128)S(1)}, f32[16,384]{1,0:T(8,128)S(1)}, u32[]{:S(2)}, u32[]{:S(2)}) collective-permute-start(f32[16,384]{1,0:T(8,128)S(1)} %get-tuple-element.156), channel_id=1, source_target_pairs={{0,6},{2,4},{4,2},{6,0},{1,7},{3,5},{5,3},{7,1},{8,14},{10,12},{12... | collective-permute-start | bytes 73736 | tf_op jit(solution)/shard_map/ppermute | solution.py:1096
  38.6 12.8 %collective-permute-start.12 = (bf16[4,48,384]{2,1,0:T(8,128)(2,1)S(1)}, bf16[4,48,384]{2,1,0:T(8,128)(2,1)S(1)}, u32[]{:S(2)}, u32[]{:S(2)}) collective-permute-start(bf16[4,48,384]{2,1,0:T(8,128)(2,1)S(1)} %get-tuple-element.319.refs_2_), channel_id=1, source_target_pairs={{0,6},{2,4},{4,2},{6,0},{1,7},{3,5},{5,3},{7,1},{8,14},{10,12},{12... | collective-permute-start | bytes 442376 | tf_op jit(solution)/shard_map/ppermute | solution.py:1096
  40.2 11.2 %collective-permute-start.11 = (bf16[4,48,384]{2,1,0:T(8,128)(2,1)S(1)}, bf16[4,48,384]{2,1,0:T(8,128)(2,1)S(1)}, u32[]{:S(2)}, u32[]{:S(2)}) collective-permute-start(bf16[4,48,384]{2,1,0:T(8,128)(2,1)S(1)} %get-tuple-element.320.refs_1_), channel_id=1, source_target_pairs={{0,4},{2,6},{4,0},{6,2},{1,5},{3,7},{5,1},{7,3},{8,12},{10,14},{12... | collective-permute-start | bytes 442376 | tf_op jit(solution)/shard_map/ppermute | solution.py:1096
  40.3 11.1 %collective-permute-start.10 = (bf16[4,48,384]{2,1,0:T(8,128)(2,1)S(1)}, bf16[4,48,384]{2,1,0:T(8,128)(2,1)S(1)}, u32[]{:S(2)}, u32[]{:S(2)}) collective-permute-start(bf16[4,48,384]{2,1,0:T(8,128)(2,1)S(1)} %get-tuple-element.321.refs_0_), channel_id=1, source_target_pairs={{0,2},{2,0},{4,6},{6,4},{1,3},{3,1},{5,7},{7,5},{8,10},{10,8},{12,... | collective-permute-start | bytes 442376 | tf_op jit(solution)/shard_map/ppermute | solution.py:1096
  51.6 26.2 %collective-permute-start.13 = (bf16[256,384]{1,0:T(8,128)(2,1)S(1)}, bf16[256,384]{1,0:T(8,128)(2,1)S(1)}, u32[]{:S(2)}, u32[]{:S(2)}) collective-permute-start(bf16[256,384]{1,0:T(8,128)(2,1)S(1)} %pad_maximum_fusion.3), channel_id=1, source_target_pairs={{0,8},{8,0},{16,24},{24,16},{1,9},{9,1},{17,25},{25,17},{2,10},{10... | collective-permute-start | bytes 589832 | tf_op jit(solution)/shard_map/ppermute | solution.py:1096
  81.0 19.2 %collective-permute-start.18 = (bf16[320,384]{1,0:T(8,128)(2,1)S(1)}, bf16[320,384]{1,0:T(8,128)(2,1)S(1)}, u32[]{:S(2)}, u32[]{:S(2)}) collective-permute-start(bf16[320,384]{1,0:T(8,128)(2,1)S(1)} %pad_maximum_fusion.2), channel_id=1, source_target_pairs={{0,16},{8,24},{16,0},{24,8},{1,17},{9,25},{17,1},{25,9},{2,18},{10... | collective-permute-start | bytes 737288 | tf_op jit(solution)/shard_map/ppermute | solution.py:1096
  83.7 16.7 %collective-permute-start.15 = (bf16[4,48,768]{2,1,0:T(8,128)(2,1)S(1)}, bf16[4,48,768]{2,1,0:T(8,128)(2,1)S(1)}, u32[]{:S(2)}, u32[]{:S(2)}) collective-permute-start(bf16[4,48,768]{2,1,0:T(8,128)(2,1)S(1)} %get-tuple-element.202), channel_id=1, source_target_pairs={{0,2},{2,0},{4,6},{6,4},{1,3},{3,1},{5,7},{7,5},{8,10},{10,8},{12,... | collective-permute-start | bytes 884744 | tf_op jit(solution)/shard_map/ppermute | solution.py:1096
  84.2 16.2 %collective-permute-start.16 = (bf16[4,48,768]{2,1,0:T(8,128)(2,1)S(1)}, bf16[4,48,768]{2,1,0:T(8,128)(2,1)S(1)}, u32[]{:S(2)}, u32[]{:S(2)}) collective-permute-start(bf16[4,48,768]{2,1,0:T(8,128)(2,1)S(1)} %get-tuple-element.203), channel_id=1, source_target_pairs={{0,4},{2,6},{4,0},{6,2},{1,5},{3,7},{5,1},{7,3},{8,12},{10,14},{12... | collective-permute-start | bytes 884744 | tf_op jit(solution)/shard_map/ppermute | solution.py:1096
  85.8 14.7 %collective-permute-start.17 = (bf16[4,48,768]{2,1,0:T(8,128)(2,1)S(1)}, bf16[4,48,768]{2,1,0:T(8,128)(2,1)S(1)}, u32[]{:S(2)}, u32[]{:S(2)}) collective-permute-start(bf16[4,48,768]{2,1,0:T(8,128)(2,1)S(1)} %get-tuple-element.204), channel_id=1, source_target_pairs={{0,6},{2,4},{4,2},{6,0},{1,7},{3,5},{5,3},{7,1},{8,14},{10,12},{12... | collective-permute-start | bytes 884744 | tf_op jit(solution)/shard_map/ppermute | solution.py:1096
  100.7 14.0 %collective-permute-start.22 = (bf16[4,48,384]{2,1,0:T(8,128)(2,1)S(1)}, bf16[4,48,384]{2,1,0:T(8,128)(2,1)S(1)}, u32[]{:S(2)}, u32[]{:S(2)}) collective-permute-start(bf16[4,48,384]{2,1,0:T(8,128)(2,1)S(1)} %fusion.8), channel_id=1, source_target_pairs={{0,6},{2,4},{4,2},{6,0},{1,7},{3,5},{5,3},{7,1},{8,14},{10,12},{12... | collective-permute-start | bytes 442376 | tf_op jit(solution)/shard_map/ppermute | solution.py:1096
  102.2 12.4 %collective-permute-start.21 = (bf16[4,48,384]{2,1,0:T(8,128)(2,1)S(1)}, bf16[4,48,384]{2,1,0:T(8,128)(2,1)S(1)}, u32[]{:S(2)}, u32[]{:S(2)}) collective-permute-start(bf16[4,48,384]{2,1,0:T(8,128)(2,1)S(1)} %fusion.8), channel_id=1, source_target_pairs={{0,4},{2,6},{4,0},{6,2},{1,5},{3,7},{5,1},{7,3},{8,12},{10,14},{12... | collective-permute-start | bytes 442376 | tf_op jit(solution)/shard_map/ppermute | solution.py:1096
  102.7 11.9 %collective-permute-start.20 = (bf16[4,48,384]{2,1,0:T(8,128)(2,1)S(1)}, bf16[4,48,384]{2,1,0:T(8,128)(2,1)S(1)}, u32[]{:S(2)}, u32[]{:S(2)}) collective-permute-start(bf16[4,48,384]{2,1,0:T(8,128)(2,1)S(1)} %fusion.8), channel_id=1, source_target_pairs={{0,2},{2,0},{4,6},{6,4},{1,3},{3,1},{5,7},{7,5},{8,10},{10,8},{12,... | collective-permute-start | bytes 442376 | tf_op jit(solution)/shard_map/ppermute | solution.py:1096
  104.2 10.3 %collective-permute-start.19 = (bf16[4,48,768]{2,1,0:T(8,128)(2,1)S(1)}, bf16[4,48,768]{2,1,0:T(8,128)(2,1)S(1)}, u32[]{:S(2)}, u32[]{:S(2)}) collective-permute-start(bf16[4,48,768]{2,1,0:T(8,128)(2,1)S(1)} %fusion.2), channel_id=1, source_target_pairs={{0,8},{8,0},{16,24},{24,16},{1,9},{9,1},{17,25},{25,17},{2,10},{10... | collective-permute-start | bytes 884744 | tf_op jit(solution)/shard_map/ppermute | solution.py:1096
  115.8 17.9 %collective-permute-start.28 = (bf16[1024,384]{1,0:T(8,128)(2,1)S(1)}, bf16[1024,384]{1,0:T(8,128)(2,1)S(1)}, u32[]{:S(2)}, u32[]{:S(2)}) collective-permute-start(bf16[1024,384]{1,0:T(8,128)(2,1)S(1)} %pad_maximum_fusion), channel_id=1, source_target_pairs={{0,1},{1,0},{2,3},{3,2},{4,5},{5,4},{6,7},{7,6},{8,9},{9,8},{10,11... | collective-permute-start | bytes 2359304 | tf_op jit(solution)/shard_map/ppermute | solution.py:1096
  115.9 16.7 %collective-permute-start.23 = (bf16[4,48,768]{2,1,0:T(8,128)(2,1)S(1)}, bf16[4,48,768]{2,1,0:T(8,128)(2,1)}, u32[]{:S(2)}, u32[]{:S(2)}) collective-permute-start(bf16[4,48,768]{2,1,0:T(8,128)(2,1)S(1)} %add_convert_fusion.1), channel_id=1, source_target_pairs={{0,16},{8,24},{16,0},{24,8},{1,17},{9,25},{17,1},{25,9},{2,18},{10... | collective-permute-start | bytes 884744 | tf_op jit(solution)/shard_map/ppermute | solution.py:1096
  119.1 14.8 %collective-permute-start.27 = (bf16[4,48,384]{2,1,0:T(8,128)(2,1)S(1)}, bf16[4,48,384]{2,1,0:T(8,128)(2,1)S(1)}, u32[]{:S(2)}, u32[]{:S(2)}) collective-permute-start(bf16[4,48,384]{2,1,0:T(8,128)(2,1)S(1)} %get-tuple-element.316), channel_id=1, source_target_pairs={{0,6},{2,4},{4,2},{6,0},{1,7},{3,5},{5,3},{7,1},{8,14},{10,12},{12... | collective-permute-start | bytes 442376 | tf_op jit(solution)/shard_map/ppermute | solution.py:1096
  120.6 13.2 %collective-permute-start.26 = (bf16[4,48,384]{2,1,0:T(8,128)(2,1)S(1)}, bf16[4,48,384]{2,1,0:T(8,128)(2,1)S(1)}, u32[]{:S(2)}, u32[]{:S(2)}) collective-permute-start(bf16[4,48,384]{2,1,0:T(8,128)(2,1)S(1)} %get-tuple-element.317), channel_id=1, source_target_pairs={{0,4},{2,6},{4,0},{6,2},{1,5},{3,7},{5,1},{7,3},{8,12},{10,14},{12... | collective-permute-start | bytes 442376 | tf_op jit(solution)/shard_map/ppermute | solution.py:1096
  120.9 13.0 %collective-permute-start.25 = (bf16[4,48,384]{2,1,0:T(8,128)(2,1)S(1)}, bf16[4,48,384]{2,1,0:T(8,128)(2,1)S(1)}, u32[]{:S(2)}, u32[]{:S(2)}) collective-permute-start(bf16[4,48,384]{2,1,0:T(8,128)(2,1)S(1)} %get-tuple-element.318), channel_id=1, source_target_pairs={{0,2},{2,0},{4,6},{6,4},{1,3},{3,1},{5,7},{7,5},{8,10},{10,8},{12,... | collective-permute-start | bytes 442376 | tf_op jit(solution)/shard_map/ppermute | solution.py:1096
  135.1 5.7 %collective-permute-start.32 = (bf16[208,384]{1,0:T(8,128)(2,1)S(1)}, bf16[208,384]{1,0:T(8,128)(2,1)S(1)}, u32[]{:S(2)}, u32[]{:S(2)}) collective-permute-start(bf16[208,384]{1,0:T(8,128)(2,1)S(1)} %pad_maximum_fusion.7), channel_id=1, source_target_pairs={{0,8},{8,0},{16,24},{24,16},{1,9},{9,1},{17,25},{25,17},{2,10},{10... | collective-permute-start | bytes 479240 | tf_op jit(solution)/shard_map/ppermute | solution.py:1096
  135.2 15.6 %collective-permute-start.31 = (bf16[4,48,768]{2,1,0:T(8,128)(2,1)S(1)}, bf16[4,48,768]{2,1,0:T(8,128)(2,1)S(1)}, u32[]{:S(2)}, u32[]{:S(2)}) collective-permute-start(bf16[4,48,768]{2,1,0:T(8,128)(2,1)S(1)} %add_convert_fusion), channel_id=1, source_target_pairs={{0,6},{2,4},{4,2},{6,0},{1,7},{3,5},{5,3},{7,1},{8,14},{10,12},{12... | collective-permute-start | bytes 884744 | tf_op jit(solution)/shard_map/ppermute | solution.py:1096
  136.7 14.3 %collective-permute-start.30 = (bf16[4,48,768]{2,1,0:T(8,128)(2,1)S(1)}, bf16[4,48,768]{2,1,0:T(8,128)(2,1)S(1)}, u32[]{:S(2)}, u32[]{:S(2)}) collective-permute-start(bf16[4,48,768]{2,1,0:T(8,128)(2,1)S(1)} %add_convert_fusion), channel_id=1, source_target_pairs={{0,4},{2,6},{4,0},{6,2},{1,5},{3,7},{5,1},{7,3},{8,12},{10,14},{12... | collective-permute-start | bytes 884744 | tf_op jit(solution)/shard_map/ppermute | solution.py:1096
  137.3 13.9 %collective-permute-start.29 = (bf16[4,48,768]{2,1,0:T(8,128)(2,1)S(1)}, bf16[4,48,768]{2,1,0:T(8,128)(2,1)S(1)}, u32[]{:S(2)}, u32[]{:S(2)}) collective-permute-start(bf16[4,48,768]{2,1,0:T(8,128)(2,1)S(1)} %add_convert_fusion), channel_id=1, source_target_pairs={{0,2},{2,0},{4,6},{6,4},{1,3},{3,1},{5,7},{7,5},{8,10},{10,8},{12,... | collective-permute-start | bytes 884744 | tf_op jit(solution)/shard_map/ppermute | solution.py:1096
  140.9 9.7 %collective-permute-start.33 = (bf16[224,384]{1,0:T(8,128)(2,1)S(1)}, bf16[224,384]{1,0:T(8,128)(2,1)S(1)}, u32[]{:S(2)}, u32[]{:S(2)}) collective-permute-start(bf16[224,384]{1,0:T(8,128)(2,1)S(1)} %pad_maximum_fusion.6), channel_id=1, source_target_pairs={{0,16},{8,24},{16,0},{24,8},{1,17},{9,25},{17,1},{25,9},{2,18},{10... | collective-permute-start | bytes 516104 | tf_op jit(solution)/shard_map/ppermute | solution.py:1096
  151.4 8.7 %collective-permute-start.36 = (bf16[256,384]{1,0:T(8,128)(2,1)S(1)}, bf16[256,384]{1,0:T(8,128)(2,1)S(1)}, u32[]{:S(2)}, u32[]{:S(2)}) collective-permute-start(bf16[256,384]{1,0:T(8,128)(2,1)S(1)} %pad_maximum_fusion.5.refs_0_), channel_id=1, source_target_pairs={{0,6},{2,4},{4,2},{6,0},{1,7},{3,5},{5,3},{7,1},{8,14},{10,12},{12... | collective-permute-start | bytes 589832 | tf_op jit(solution)/shard_map/ppermute | solution.py:1096
  152.8 11.0 %collective-permute-start.35 = (bf16[256,384]{1,0:T(8,128)(2,1)S(1)}, bf16[256,384]{1,0:T(8,128)(2,1)S(1)}, u32[]{:S(2)}, u32[]{:S(2)}) collective-permute-start(bf16[256,384]{1,0:T(8,128)(2,1)S(1)} %pad_maximum_fusion.5.refs_0_), channel_id=1, source_target_pairs={{0,4},{2,6},{4,0},{6,2},{1,5},{3,7},{5,1},{7,3},{8,12},{10,14},{12... | collective-permute-start | bytes 589832 | tf_op jit(solution)/shard_map/ppermute | solution.py:1096
  153.4 10.4 %collective-permute-start.34 = (bf16[256,384]{1,0:T(8,128)(2,1)S(1)}, bf16[256,384]{1,0:T(8,128)(2,1)S(1)}, u32[]{:S(2)}, u32[]{:S(2)}) collective-permute-start(bf16[256,384]{1,0:T(8,128)(2,1)S(1)} %pad_maximum_fusion.5.refs_0_), channel_id=1, source_target_pairs={{0,2},{2,0},{4,6},{6,4},{1,3},{3,1},{5,7},{7,5},{8,10},{10,8},{12,... | collective-permute-start | bytes 589832 | tf_op jit(solution)/shard_map/ppermute | solution.py:1096
  (57 other events, 328.6 us)
